TPU v7x, 256 devices: a whole 4x4x8 slice. The times are simulated.
256 devices in a mesh: lat: 8 (over y_hi, x), lon: 32 (over y_lo, z, core).
Axes of the slice: x: 4, y: 4 (y_hi: 2, y_lo: 2; y = y_hi * 2 + y_lo), z: 8, core: 2. Of those that a mesh axis runs over, the one named last changes fastest.
Arguments:
- thermal_anomaly: float32 [8, 512, 4096], P(None, 'lat', 'lon'), may hold values from -6 to 6
- saltiness_anomaly: float32 [8, 512, 4096], P(None, 'lat', 'lon'), may hold values from -6 to 6
- eastward_flow_speed: float32 [8, 512, 4096], P(None, 'lat', 'lon'), may hold values from -3 to 3
- northward_flow_speed: float32 [8, 512, 4096], P(None, 'lat', 'lon'), may hold values from -3 to 3
- sea_indicator_field: int32 [8, 512, 4096], P(None, 'lat', 'lon'), may hold values 0 or 1
Outputs:
- temperature_out: float32 [8, 512, 4096], P(None, 'lat', 'lon')
- salinity_out: float32 [8, 512, 4096], P(None, 'lat', 'lon')
- zonal_out: float32 [8, 512, 4096], P(None, 'lat', 'lon')
- merid_out: float32 [8, 512, 4096], P(None, 'lat', 'lon')
All inputs are finite; a program needn't handle non-finite values. No bound on the sum of `sea_indicator_field` on one device may be relied on, other than what follows from the above.
Results may differ from a plain program's by a relative error of at most 0.00002.
Values sent between devices are 32-bit elements; how exact they have to be, the bound alone decides.
No kernel may reach another device: no remote copies, remote signals or barrier semaphores. Data moves between devices by JAX's collectives and lax.ppermute only.
A program may use at most 64 MiB of HBM per device.

v0:
```python
import functools

import jax
import jax.numpy as jnp
from jax import lax
from jax.experimental import pallas as pl
from jax.experimental.pallas import tpu as pltpu
from jax.sharding import PartitionSpec as P

NSUB = 4
LEVELS = 8
ROWS = 64
LANES = 128
CHUNKS = ROWS // 8
AXES = ("lat", "lon")

FACE = 0.08
PSCALE = 0.15 / 0.08
ASCALE = 0.0625 / 0.08
DRAG = 0.05
VMEM = 48 * 1024 * 1024


def lane_roll(x, amount):
    amount %= LANES
    return x if amount == 0 else pltpu.roll(x, amount, axis=x.ndim - 1)


def row_roll(x, amount):
    return pltpu.roll(x, amount, axis=x.ndim - 2)


def lane_index(rows=8):
    return lax.broadcasted_iota(jnp.int32, (rows, LANES), 1)


def row_index():
    return lax.broadcasted_iota(jnp.int32, (8, LANES), 0)


def density_tenth(temper, salt, depth):
    c = PSCALE * 0.1
    return salt * (c * 0.8 + (c * 0.03) * temper) - temper * (
        (c * 0.25 + c * 0.1 * depth) + (c * 0.06) * temper
    )


def along_faces(k, now, nxt, normal, press_now, press_nxt):
    t0, s0, t1, s1 = now[0], now[1], nxt[0], nxt[1]
    a = ASCALE * (now[normal] + nxt[normal])
    less = k * (1.0 - a)
    more = k * (1.0 + a)
    ft = less * t1 - more * t0
    fs = less * s1 - more * s0
    dn = nxt[normal] - now[normal]
    dp = press_nxt - press_now
    tang = 5 - normal
    ftang = k * (nxt[tang] - now[tang])
    ahead = k * (dn - dp)
    behind = k * (dn + dp)
    return ft, fs, ftang, ahead, behind


def combine(now, ocean, coriolis, east, west, north, south):
    t, s, u, v = now
    nt = t + ((east[0] - west[0]) + (north[0] - south[0]))
    ns = s + ((east[1] - west[1]) + (north[1] - south[1]))
    nu = u + (ocean * (coriolis * v - DRAG * u) + ((east[3] - west[4]) + (north[2] - south[2])))
    nv = v + (ocean * (-coriolis * u - DRAG * v) + ((east[2] - west[2]) + (north[3] - south[4])))
    return nt, ns, nu, nv


def coriolis_rows(first_row, total, shape, start):
    row = first_row + start + lax.broadcasted_iota(jnp.int32, shape, len(shape) - 2)
    row = jnp.where(row >= total, 2 * total - 1 - row, row).astype(jnp.float32)
    return 0.1 + 0.3 * (row + 0.5) / total


def pack_rows_body(count, *refs):
    low, high, (to_a, to_b) = refs[:5], refs[5:10], refs[10:]
    odd = lax.rem(lax.axis_index("lat"), 2) == 1
    upper = row_index() < 4
    for f in range(5):
        for m in range(LEVELS // 2):
            b0, b1 = low[f][2 * m], low[f][2 * m + 1]
            t0, t1 = high[f][2 * m], high[f][2 * m + 1]
            if f == 4:
                b0, b1, t0, t1 = (w.astype(jnp.float32) for w in (b0, b1, t0, t1))
            bottom = jnp.where(upper, b0, row_roll(b1, 4))
            top = jnp.where(upper, row_roll(t0, 4), t1)
            to_a[f, m] = jnp.where(odd, bottom, top)
            to_b[f, m] = jnp.where(odd, top, bottom)


def pack_rows(fields):
    lows = [pl.BlockSpec((LEVELS, 8, LANES), lambda i: (0, 0, 0)) for _ in fields]
    highs = [pl.BlockSpec((LEVELS, 8, LANES), lambda i: (0, CHUNKS - 1, 0)) for _ in fields]
    out = jax.ShapeDtypeStruct((5, LEVELS // 2, 8, LANES), jnp.float32)
    return pl.pallas_call(
        functools.partial(pack_rows_body, 0),
        grid=(1,),
        in_specs=lows + highs,
        out_specs=[pl.BlockSpec(out.shape, lambda i: (0, 0, 0, 0))] * 2,
        out_shape=[out, out],
        name="pack_rows",
    )(*fields, *fields)


def strip_of(levels):
    lane = lane_index()
    place = lane % 32
    group = lane // 32
    total = jnp.zeros((8, LANES), jnp.float32)
    for g, block in enumerate(levels):
        east = lane_roll(block, 32 * g + 4 - 120)
        west = lane_roll(block, 32 * g + 20)
        mine = group == g
        total = jnp.where(mine & (place >= 4) & (place < 12), east, total)
        total = jnp.where(mine & (place >= 20) & (place < 28), west, total)
    return total


def squeeze(tiles, start):
    place = lane_index() % 32
    total = jnp.zeros((8, LANES), jnp.float32)
    for n, tile in enumerate(tiles):
        if tile is None:
            continue
        total = jnp.where((place >= 4 * n) & (place < 4 * n + 4), lane_roll(tile, 4 * n - start), total)
    return total


def pack_columns_body(*refs):
    fields, (strips, to_e, to_w) = refs[:5], refs[5:]
    slots = {}
    for i in range(CHUNKS):
        rows = pl.ds(8 * i, 8)
        tiles = []
        for f in range(5):
            for t in range(2):
                tile = strip_of([fields[f][4 * t + g, rows].astype(jnp.float32) for g in range(4)])
                strips[f, t, rows] = tile
                tiles.append(tile)
        to_e[i] = squeeze(tiles[:8], 8)
        to_w[i] = squeeze(tiles[:8], 20)
        slots.setdefault(i // 4, []).extend(tiles[8:])
    for j in range(CHUNKS // 4):
        to_e[CHUNKS + j] = squeeze(slots[j], 8)
        to_w[CHUNKS + j] = squeeze(slots[j], 20)


def pack_columns(fields):
    part = jax.ShapeDtypeStruct((CHUNKS + CHUNKS // 4, 8, LANES), jnp.float32)
    return pl.pallas_call(
        pack_columns_body,
        out_shape=[jax.ShapeDtypeStruct((5, 2, ROWS, LANES), jnp.float32), part, part],
        compiler_params=pltpu.CompilerParams(vmem_limit_bytes=VMEM),
        cost_estimate=pl.CostEstimate(flops=20_000_000, bytes_accessed=2_000_000, transcendentals=0),
        name="pack_columns",
    )(*fields)


def mirrored(x):
    row, lane = row_index(), lane_index()
    for bit in (1, 2):
        x = jnp.where((row & bit) == 0, row_roll(x, 8 - bit), row_roll(x, bit))
    for bit in (1, 2, 4, 8, 16, 32):
        x = jnp.where((lane & bit) == 0, lane_roll(x, -bit), lane_roll(x, bit))
    return lane_roll(x, 64)


def assemble_body(from_a, from_b, part_e, part_w, halo, strips, to_e, to_w):
    lat = lax.axis_index("lat")
    odd = lax.rem(lat, 2) == 1
    at_top = lat == lax.axis_size("lat") - 1
    upper = row_index() < 4

    @pl.when(at_top)
    def _():
        for f in range(5):
            for m in range(LEVELS // 2):
                south = row_roll(from_a[f, m], 4)
                north = mirrored(from_b[f, m])
                if f in (2, 3):
                    north = -north
                halo[f, 2 * m] = jnp.where(upper, north, south)
                halo[f, 2 * m + 1] = jnp.where(upper, row_roll(north, 4), row_roll(south, 4))

    @pl.when(jnp.logical_not(at_top))
    def _():
        for f in range(5):
            for m in range(LEVELS // 2):
                a, b = from_a[f, m], from_b[f, m]
                north = jnp.where(odd, b, a)
                south = row_roll(jnp.where(odd, a, b), 4)
                halo[f, 2 * m] = jnp.where(upper, north, south)
                halo[f, 2 * m + 1] = jnp.where(upper, row_roll(north, 4), row_roll(south, 4))

    tiles = []
    for f in range(5):
        for t in range(2):
            tile = strip_of([halo[f, 4 * t + g] for g in range(4)])
            strips[f, t] = tile
            tiles.append(tile)
    for part, out, start in ((part_e, to_e, 8), (part_w, to_w, 20)):
        for i in range(CHUNKS):
            out[i] = part[i]
        out[CHUNKS] = squeeze(tiles[:8], start)
        for j in range(CHUNKS // 4):
            out[CHUNKS + 1 + j] = part[CHUNKS + j]
        out[CHUNKS + 1 + CHUNKS // 4] = squeeze(tiles[8:], start)


def assemble(from_a, from_b, part_e, part_w):
    whole = jax.ShapeDtypeStruct((CHUNKS + 2 + CHUNKS // 4, 8, LANES), jnp.float32)
    return pl.pallas_call(
        assemble_body,
        out_shape=[
            jax.ShapeDtypeStruct((5, LEVELS, 8, LANES), jnp.float32),
            jax.ShapeDtypeStruct((5, 2, 8, LANES), jnp.float32),
            whole,
            whole,
        ],
        name="assemble",
    )(from_a, from_b, part_e, part_w)


PADDED = ROWS + 16
TALL = PADDED + 8


def main_body(*refs):
    fields, halo, outs = refs[:5], refs[5], refs[6:10]
    state, press, face_e, face_n, wet, past, turn = refs[10:]
    lat = lax.axis_index("lat")
    total = ROWS * lax.axis_size("lat")
    turn[...] = coriolis_rows(lat * ROWS, total, (PADDED, LANES), -8)

    def load_in(k, _):
        for f in range(4):
            state[0, f, k, 0:8] = halo[f, k]
            state[0, f, k, 8 : 8 + ROWS] = fields[f][k]
            state[0, f, k, 8 + ROWS : PADDED] = halo[f, k]
        wet[k, 0:8] = halo[4, k]
        wet[k, 8 : 8 + ROWS] = fields[4][k].astype(jnp.float32)
        wet[k, 8 + ROWS : PADDED] = halo[4, k]
        return 0

    lax.fori_loop(0, LEVELS, load_in, 0)

    def load_faces(k, _):
        here = wet[k, 0:PADDED]
        face_e[k] = FACE * (here * lane_roll(here, -1))
        face_n[k] = FACE * (here * wet[k, 1 : PADDED + 1])
        return 0

    lax.fori_loop(0, LEVELS, load_faces, 0)

    def pressure(src, i, _):
        rows = pl.ds(pl.multiple_of(8 * i, 8), 8)
        base = jnp.zeros((8, LANES), jnp.float32)
        for k in range(LEVELS):
            h = density_tenth(state[src, 0, k, rows], state[src, 1, k, rows], (k + 0.5) / LEVELS)
            base = base + h
            press[k, rows] = base
            base = base + h
        return 0

    def northern(src, k, i, now, p0):
        after = pl.ds(8 * i + 1, 8)
        nxt = [state[src, f, k, after] for f in range(4)]
        return along_faces(face_n[k, pl.ds(8 * i, 8)], now, nxt, 3, p0, press[k, after])

    def update(src, store, i, _):
        rows = pl.ds(8 * i, 8)
        f = turn[rows]
        for k in range(LEVELS):
            now = [state[src, q, k, rows] for q in range(4)]
            p0 = press[k, rows]
            east = along_faces(
                face_e[k, rows], now, [lane_roll(q, -1) for q in now], 2, p0, lane_roll(p0, -1)
            )
            west = [
                lane_roll(east[0], 1),
                lane_roll(east[1], 1),
                lane_roll(east[2], 1),
                None,
                lane_roll(east[4], 1),
            ]
            north = northern(src, k, i, now, p0)
            for n in (0, 1, 2, 4):
                past[n, k, pl.ds(8 + 8 * i, 8)] = north[n]
            south = [None if n == 3 else past[n, k, pl.ds(7 + 8 * i, 8)] for n in range(5)]
            store(k, i, combine(now, wet[k, rows], f, east, west, north, south))
        return 0

    for step in range(NSUB):
        src = step % 2
        for i in range(CHUNKS + 2):
            pressure(src, i, 0)
        if step < NSUB - 1:

            def store(k, i, new):
                for q in range(4):
                    state[1 - src, q, k, pl.ds(8 * i, 8)] = new[q]

            for i in range(CHUNKS + 2):
                update(src, store, i, 0)
        else:

            def store(k, i, new):
                for q in range(4):
                    outs[q][k, pl.ds(8 * (i - 1), 8)] = new[q]

            for k in range(LEVELS):
                now = [state[src, q, k, 0:8] for q in range(4)]
                north = northern(src, k, 0, now, press[k, 0:8])
                for n in (0, 1, 2, 4):
                    past[n, k, 8:16] = north[n]
            for i in range(1, CHUNKS + 1):
                update(src, store, i, 0)


def main_block(fields, halo):
    out = jax.ShapeDtypeStruct((LEVELS, ROWS, LANES), jnp.float32)
    f32 = jnp.float32
    return pl.pallas_call(
        main_body,
        out_shape=[out] * 4,
        scratch_shapes=[
            pltpu.VMEM((2, 4, LEVELS, TALL, LANES), f32),
            pltpu.VMEM((LEVELS, TALL, LANES), f32),
            pltpu.VMEM((LEVELS, PADDED, LANES), f32),
            pltpu.VMEM((LEVELS, PADDED, LANES), f32),
            pltpu.VMEM((LEVELS, TALL, LANES), f32),
            pltpu.VMEM((5, LEVELS, TALL, LANES), f32),
            pltpu.VMEM((PADDED, LANES), f32),
        ],
        compiler_params=pltpu.CompilerParams(vmem_limit_bytes=VMEM),
        cost_estimate=pl.CostEstimate(flops=300_000_000, bytes_accessed=20_000_000, transcendentals=0),
        name="main_block",
    )(*fields, halo)


def strips_body(own, own_halo, from_w, from_e, *refs):
    mains, outs = refs[:4], refs[4:8]
    state, wet, turn = refs[8:]
    lat = lax.axis_index("lat")
    total = ROWS * lax.axis_size("lat")
    turn[...] = coriolis_rows(lat * ROWS, total, (PADDED, LANES), -8)
    place = lane_index() % 32
    halo_w = (place >= 16) & (place < 20)
    halo_e = (place >= 12) & (place < 16)

    def put(f, t, i, tile):
        targets = [1 + i] if i < CHUNKS else [0, CHUNKS + 1]
        for c in targets:
            if f < 4:
                state[0, f, t, 8 * c : 8 * c + 8] = tile
            else:
                wet[t, 8 * c : 8 * c + 8] = tile

    for i in range(CHUNKS + 1):
        for f in range(5):
            for t in range(2):
                tile = own[f, t, 8 * i : 8 * i + 8] if i < CHUNKS else own_halo[f, t]
                if f < 4:
                    slot, chunk = 2 * f + t, i
                else:
                    slot, chunk = 2 * (i % 4) + t, CHUNKS + 1 + i // 4
                tile = jnp.where(halo_w, lane_roll(from_w[chunk], 16 - 4 * slot), tile)
                tile = jnp.where(halo_e, lane_roll(from_e[chunk], 12 - 4 * slot), tile)
                put(f, t, i, tile)

    lane = lane_index(PADDED)
    group = lane // 32

    for step in range(NSUB):
        src = step % 2
        press = []
        whole = None
        for t in range(2):
            depth = (4 * t + group + 0.5) / LEVELS
            h = density_tenth(state[src, 0, t, 0:PADDED], state[src, 1, t, 0:PADDED], depth)
            inc = h + jnp.where(group >= 1, lane_roll(h, 32), 0.0)
            inc = inc + jnp.where(group >= 2, lane_roll(inc, 64), 0.0)
            p = 2.0 * inc - h
            if t == 0:
                whole = h + lane_roll(h, 32)
                whole = whole + lane_roll(whole, 64)
            else:
                p = p + 2.0 * whole
            press.append(p)
        for t in range(2):
            now = [state[src, f, t, 0:PADDED] for f in range(4)]
            here = wet[t, 0:PADDED]
            up = lambda q: row_roll(q, PADDED - 1)
            down = lambda q: row_roll(q, 1)
            east_face = FACE * (here * lane_roll(here, -1))
            north_face = FACE * (here * up(here))
            p0 = press[t]
            east = along_faces(east_face, now, [lane_roll(q, -1) for q in now], 2, p0, lane_roll(p0, -1))
            west = [lane_roll(q, 1) for q in east]
            north = along_faces(north_face, now, [up(q) for q in now], 3, p0, up(p0))
            south = [down(q) for q in north]
            new = combine(now, here, turn[...], east, west, north, south)
            for f in range(4):
                state[1 - src, f, t, 0:PADDED] = new[f]

    src = NSUB % 2
    lane = lane_index(ROWS)
    for f in range(4):
        for k in range(LEVELS):
            tile = state[src, f, k // 4, 8 : 8 + ROWS]
            g = 32 * (k % 4)
            block = mains[f][k]
            block = jnp.where(lane < 4, lane_roll(tile, -(g + 20)), block)
            block = jnp.where(lane >= LANES - 4, lane_roll(tile, 124 - (g + 8)), block)
            outs[f][k] = block


def strips_and_merge(own, own_halo, from_w, from_e, mains):
    out = jax.ShapeDtypeStruct((LEVELS, ROWS, LANES), jnp.float32)
    f32 = jnp.float32
    return pl.pallas_call(
        strips_body,
        out_shape=[out] * 4,
        scratch_shapes=[
            pltpu.VMEM((2, 4, 2, PADDED, LANES), f32),
            pltpu.VMEM((2, PADDED, LANES), f32),
            pltpu.VMEM((PADDED, LANES), f32),
        ],
        compiler_params=pltpu.CompilerParams(vmem_limit_bytes=VMEM),
        name="strips_and_merge",
    )(own, own_halo, from_w, from_e, *mains)


def lat_routes(lats, lons):
    first, second = [], []
    for j in range(lons):
        for i in range(lats):
            first.append((i * lons + j, (i ^ 1) * lons + j))
        for i in range(1, lats - 1):
            other = i + 1 if i % 2 else i - 1
            second.append((i * lons + j, other * lons + j))
        second.append(((lats - 1) * lons + j, (lats - 1) * lons + lons - 1 - j))
    return first, second


def on_device(*args):
    lats, lons = lax.axis_size("lat"), lax.axis_size("lon")
    route_a, route_b = lat_routes(lats, lons)
    to_a, to_b = pack_rows(args)
    from_b = lax.ppermute(to_b, AXES, route_b)
    from_a = lax.ppermute(to_a, AXES, route_a)
    own, part_e, part_w = pack_columns(args)
    halo, own_halo, to_e, to_w = assemble(from_a, from_b, part_e, part_w)
    from_w = lax.ppermute(to_e, "lon", [(i, (i + 1) % lons) for i in range(lons)])
    from_e = lax.ppermute(to_w, "lon", [((i + 1) % lons, i) for i in range(lons)])
    mains = main_block(args, halo)
    return tuple(strips_and_merge(own, own_halo, from_w, from_e, mains))


def solution(mesh):
    spec = P(None, "lat", "lon")
    return jax.shard_map(
        on_device,
        mesh=mesh,
        in_specs=(spec,) * 5,
        out_specs=(spec,) * 4,
        check_vma=False,
    )
```

profile of v0, /device:TPU:22, one launch (start us, length us, event | category | flops | bytes accessed | tf_op | source)
XLA Modules:
  0.0 51.9 jit_solution(4366542131811596510)
XLA Ops:
  0.6 0.0 copy-start.4
  0.6 0.0 copy-start.3
  0.7 0.0 copy-start.2
  0.7 0.0 copy-start.1
  0.7 0.0 copy-start
  0.7 1.7 %pack_rows.1 = (f32[5,4,8,128]{3,2,1,0:T(8,128)}, f32[5,4,8,128]{3,2,1,0:T(8,128)}) custom-call(f32[8,64,128]{2,1,0:T(8,128)} %refs_0_.5, f32[8,64,128]{2,1,0:T(8,128)} %refs_1_.5, f32[8,64,128]{2,1,0:T(8,128)} %refs_2_.5, f32[8,64,128]{2,1,0:T(8,128)} %refs_3_.5, s32[8,64,128]{2,1,0:T(8,128)} %refs_4_.5, f32[8,64,128]{2,1,0:T(8,128)} %refs_0_.5, ...), custom_call_target="tpu_custom_call" | custom-call | tf_op jit(solution)/shard_map/pack_rows/pallas_call | solution.py:99
  2.4 0.8 %collective-permute-start = (f32[5,4,8,128]{3,2,1,0:T(8,128)}, f32[5,4,8,128]{3,2,1,0:T(8,128)S(1)}, u32[]{:S(2)}, u32[]{:S(2)}) collective-permute-start(f32[5,4,8,128]{3,2,1,0:T(8,128)} %get-tuple-element.18), channel_id=1, source_target_pairs={{0,32},{32,0},{64,96},{96,64},{128,160},{160,128},{192,224},{224,1... | collective-permute-start | bytes 245768 | tf_op jit(solution)/shard_map/ppermute | solution.py:455
  3.2 7.6 %collective-permute-start.1 = (f32[5,4,8,128]{3,2,1,0:T(8,128)}, f32[5,4,8,128]{3,2,1,0:T(8,128)S(1)}, u32[]{:S(2)}, u32[]{:S(2)}) collective-permute-start(f32[5,4,8,128]{3,2,1,0:T(8,128)} %get-tuple-element.19), channel_id=1, source_target_pairs={{32,64},{64,32},{96,128},{128,96},{160,192},{192,160},{224,255},{3... | collective-permute-start | bytes 245768 | tf_op jit(solution)/shard_map/ppermute | solution.py:454
  10.8 0.0 copy-done.4
  10.9 0.0 copy-done.3
  10.9 0.0 copy-done.2
  10.9 0.0 copy-done.1
  10.9 0.0 copy-done
  10.9 1.2 %pack_columns.1 = (f32[5,2,64,128]{3,2,1,0:T(8,128)S(1)}, f32[10,8,128]{2,1,0:T(8,128)S(1)}, f32[10,8,128]{2,1,0:T(8,128)S(1)}) custom-call(f32[8,64,128]{2,1,0:T(8,128)S(1)} %copy-done, f32[8,64,128]{2,1,0:T(8,128)S(1)} %copy-done.1, f32[8,64,128]{2,1,0:T(8,128)S(1)} %copy-done.2, f32[8,64,128]{2,1,0:T(8,128)S(1)} %copy-done.3, s32[8,64,128]{2,1,0:T(8,128)S(1)} %copy-done.4), custom_call_target="tpu_custom_call" | custom-call | flops 20000000 | bytes 2000000 | tf_op jit(solution)/shard_map/pack_columns/pallas_call | solution.py:154
  12.1 0.0 copy-start.7
  12.2 0.6 %copy-done.7 = f32[10,8,128]{2,1,0:T(8,128)} copy-done((f32[10,8,128]{2,1,0:T(8,128)}, f32[10,8,128]{2,1,0:T(8,128)S(1)}, u32[]{:S(2)}) %copy-start.7) | copy-done | bytes 40984
  12.8 0.0 copy-start.8
  12.8 0.6 %copy-done.8 = f32[10,8,128]{2,1,0:T(8,128)} copy-done((f32[10,8,128]{2,1,0:T(8,128)}, f32[10,8,128]{2,1,0:T(8,128)S(1)}, u32[]{:S(2)}) %copy-start.8) | copy-done | bytes 40984
  13.4 0.0 collective-permute-done.from_a
  13.4 0.0 copy-start.9
  13.4 1.9 %collective-permute-done.1.from_b = f32[5,4,8,128]{3,2,1,0:T(8,128)S(1)} collective-permute-done((f32[5,4,8,128]{3,2,1,0:T(8,128)}, f32[5,4,8,128]{3,2,1,0:T(8,128)S(1)}, u32[]{:S(2)}, u32[]{:S(2)}) %collective-permute-start.1) | collective-permute-done | bytes 81952 | tf_op jit(solution)/shard_map/ppermute | solution.py:454
  15.2 0.0 copy-start.10
  15.2 0.0 copy-done.9
  15.2 0.6 %copy-done.10 = f32[5,4,8,128]{3,2,1,0:T(8,128)} copy-done((f32[5,4,8,128]{3,2,1,0:T(8,128)}, f32[5,4,8,128]{3,2,1,0:T(8,128)S(1)}, u32[]{:S(2)}) %copy-start.10) | copy-done | bytes 81944
  15.9 2.3 %assemble.1 = (f32[5,8,8,128]{3,2,1,0:T(8,128)}, f32[5,2,8,128]{3,2,1,0:T(8,128)}, f32[12,8,128]{2,1,0:T(8,128)}, f32[12,8,128]{2,1,0:T(8,128)}) custom-call(f32[5,4,8,128]{3,2,1,0:T(8,128)} %copy-done.9, f32[5,4,8,128]{3,2,1,0:T(8,128)} %copy-done.10, f32[10,8,128]{2,1,0:T(8,128)} %copy-done.7, f32[10,8,128]{2,1,0:T(8,128)} %copy-done.8), custom_call_target="tpu_custom_call" | custom-call | tf_op jit(solution)/shard_map/assemble/pallas_call | solution.py:216
  18.2 0.6 %collective-permute-start.2 = (f32[12,8,128]{2,1,0:T(8,128)}, f32[12,8,128]{2,1,0:T(8,128)S(1)}, u32[]{:S(2)}, u32[]{:S(2)}) collective-permute-start(f32[12,8,128]{2,1,0:T(8,128)} %get-tuple-element.23), channel_id=1, source_target_pairs={{0,1},{1,2},{2,3},{3,4},{4,5},{5,6},{6,7},{7,8},{8,9},{9,10},{10,1... | collective-permute-start | bytes 147464 | tf_op jit(solution)/shard_map/ppermute | solution.py:458
  18.8 3.9 %collective-permute-start.3 = (f32[12,8,128]{2,1,0:T(8,128)}, f32[12,8,128]{2,1,0:T(8,128)S(1)}, u32[]{:S(2)}, u32[]{:S(2)}) collective-permute-start(f32[12,8,128]{2,1,0:T(8,128)} %get-tuple-element.24), channel_id=1, source_target_pairs={{1,0},{2,1},{3,2},{4,3},{5,4},{6,5},{7,6},{8,7},{9,8},{10,9},{11,1... | collective-permute-start | bytes 147464 | tf_op jit(solution)/shard_map/ppermute | solution.py:459
  22.8 0.0 copy-start.5
  22.8 0.9 %copy-done.5 = f32[5,8,8,128]{3,2,1,0:T(8,128)S(1)} copy-done((f32[5,8,8,128]{3,2,1,0:T(8,128)S(1)}, f32[5,8,8,128]{3,2,1,0:T(8,128)}, u32[]{:S(2)}) %copy-start.5) | copy-done | bytes 163864
  23.7 0.0 copy-start.6
  23.7 24.7 %main_block.1 = (f32[8,64,128]{2,1,0:T(8,128)S(1)}, f32[8,64,128]{2,1,0:T(8,128)S(1)}, f32[8,64,128]{2,1,0:T(8,128)S(1)}, f32[8,64,128]{2,1,0:T(8,128)S(1)}) custom-call(f32[8,64,128]{2,1,0:T(8,128)S(1)} %copy-done, f32[8,64,128]{2,1,0:T(8,128)S(1)} %copy-done.1, f32[8,64,128]{2,1,0:T(8,128)S(1)} %copy-done.2, f32[8,64,128]{2,1,0:T(8,128)S(1)} %copy-done.3, ...), custom_call_target="tpu_custom_call" | custom-call | flops 300000000 | bytes 20000000 | tf_op jit(solution)/shard_map/main_block/pallas_call | solution.py:327
  48.4 0.0 collective-permute-done.2.from_w
  48.4 0.0 collective-permute-done.3.from_e
  48.4 0.0 copy-done.6
  48.4 3.5 %strips_and_merge.1 = (f32[8,64,128]{2,1,0:T(8,128)}, f32[8,64,128]{2,1,0:T(8,128)}, f32[8,64,128]{2,1,0:T(8,128)}, f32[8,64,128]{2,1,0:T(8,128)}) custom-call(f32[5,2,64,128]{3,2,1,0:T(8,128)S(1)} %get-tuple-element.17.own, f32[5,2,8,128]{3,2,1,0:T(8,128)S(1)} %copy-done.6, f32[12,8,128]{2,1,0:T(8,128)S(1)} %collective-permute-done.2.from_w, ...), custom_call_target="tpu_custom_call" | custom-call | tf_op jit(solution)/shard_map/strips_and_merge/pallas_call | solution.py:425
Async XLA Ops:
  0.6 10.2 %copy-start.4 = (s32[8,64,128]{2,1,0:T(8,128)S(1)}, s32[8,64,128]{2,1,0:T(8,128)}, u32[]{:S(2)}) copy-start(s32[8,64,128]{2,1,0:T(8,128)} %refs_4_.5) | copy-start | bytes 786436
  0.6 10.2 %copy-start.3 = (f32[8,64,128]{2,1,0:T(8,128)S(1)}, f32[8,64,128]{2,1,0:T(8,128)}, u32[]{:S(2)}) copy-start(f32[8,64,128]{2,1,0:T(8,128)} %refs_3_.5) | copy-start | bytes 786436
  0.7 10.2 %copy-start.2 = (f32[8,64,128]{2,1,0:T(8,128)S(1)}, f32[8,64,128]{2,1,0:T(8,128)}, u32[]{:S(2)}) copy-start(f32[8,64,128]{2,1,0:T(8,128)} %refs_2_.5) | copy-start | bytes 786436
  0.7 10.2 %copy-start.1 = (f32[8,64,128]{2,1,0:T(8,128)S(1)}, f32[8,64,128]{2,1,0:T(8,128)}, u32[]{:S(2)}) copy-start(f32[8,64,128]{2,1,0:T(8,128)} %refs_1_.5) | copy-start | bytes 786436
  0.7 10.2 %copy-start = (f32[8,64,128]{2,1,0:T(8,128)S(1)}, f32[8,64,128]{2,1,0:T(8,128)}, u32[]{:S(2)}) copy-start(f32[8,64,128]{2,1,0:T(8,128)} %refs_0_.5) | copy-start | bytes 786436
  2.4 11.0 %collective-permute-start = (f32[5,4,8,128]{3,2,1,0:T(8,128)}, f32[5,4,8,128]{3,2,1,0:T(8,128)S(1)}, u32[]{:S(2)}, u32[]{:S(2)}) collective-permute-start(f32[5,4,8,128]{3,2,1,0:T(8,128)} %get-tuple-element.18), channel_id=1, source_target_pairs={{0,32},{32,0},{64,96},{96,64},{128,160},{160,128},{192,224},{224,1... | collective-permute-start | bytes 245768 | tf_op jit(solution)/shard_map/ppermute | solution.py:455
  3.2 12.0 %collective-permute-start.1 = (f32[5,4,8,128]{3,2,1,0:T(8,128)}, f32[5,4,8,128]{3,2,1,0:T(8,128)S(1)}, u32[]{:S(2)}, u32[]{:S(2)}) collective-permute-start(f32[5,4,8,128]{3,2,1,0:T(8,128)} %get-tuple-element.19), channel_id=1, source_target_pairs={{32,64},{64,32},{96,128},{128,96},{160,192},{192,160},{224,255},{3... | collective-permute-start | bytes 245768 | tf_op jit(solution)/shard_map/ppermute | solution.py:454
  12.1 0.6 %copy-start.7 = (f32[10,8,128]{2,1,0:T(8,128)}, f32[10,8,128]{2,1,0:T(8,128)S(1)}, u32[]{:S(2)}) copy-start(f32[10,8,128]{2,1,0:T(8,128)S(1)} %get-tuple-element.20.part_e) | copy-start | bytes 122884
  12.8 0.6 %copy-start.8 = (f32[10,8,128]{2,1,0:T(8,128)}, f32[10,8,128]{2,1,0:T(8,128)S(1)}, u32[]{:S(2)}) copy-start(f32[10,8,128]{2,1,0:T(8,128)S(1)} %get-tuple-element.21.part_w) | copy-start | bytes 122884
  13.4 1.9 %copy-start.9 = (f32[5,4,8,128]{3,2,1,0:T(8,128)}, f32[5,4,8,128]{3,2,1,0:T(8,128)S(1)}, u32[]{:S(2)}) copy-start(f32[5,4,8,128]{3,2,1,0:T(8,128)S(1)} %collective-permute-done.from_a) | copy-start | bytes 245764
  15.2 0.6 %copy-start.10 = (f32[5,4,8,128]{3,2,1,0:T(8,128)}, f32[5,4,8,128]{3,2,1,0:T(8,128)S(1)}, u32[]{:S(2)}) copy-start(f32[5,4,8,128]{3,2,1,0:T(8,128)S(1)} %collective-permute-done.1.from_b) | copy-start | bytes 245764
  18.2 30.2 %collective-permute-start.2 = (f32[12,8,128]{2,1,0:T(8,128)}, f32[12,8,128]{2,1,0:T(8,128)S(1)}, u32[]{:S(2)}, u32[]{:S(2)}) collective-permute-start(f32[12,8,128]{2,1,0:T(8,128)} %get-tuple-element.23), channel_id=1, source_target_pairs={{0,1},{1,2},{2,3},{3,4},{4,5},{5,6},{6,7},{7,8},{8,9},{9,10},{10,1... | collective-permute-start | bytes 147464 | tf_op jit(solution)/shard_map/ppermute | solution.py:458
  18.8 29.5 %collective-permute-start.3 = (f32[12,8,128]{2,1,0:T(8,128)}, f32[12,8,128]{2,1,0:T(8,128)S(1)}, u32[]{:S(2)}, u32[]{:S(2)}) collective-permute-start(f32[12,8,128]{2,1,0:T(8,128)} %get-tuple-element.24), channel_id=1, source_target_pairs={{1,0},{2,1},{3,2},{4,3},{5,4},{6,5},{7,6},{8,7},{9,8},{10,9},{11,1... | collective-permute-start | bytes 147464 | tf_op jit(solution)/shard_map/ppermute | solution.py:459
  22.8 0.9 %copy-start.5 = (f32[5,8,8,128]{3,2,1,0:T(8,128)S(1)}, f32[5,8,8,128]{3,2,1,0:T(8,128)}, u32[]{:S(2)}) copy-start(f32[5,8,8,128]{3,2,1,0:T(8,128)} %get-tuple-element.25.refs_5_) | copy-start | bytes 491524
  23.7 24.7 %copy-start.6 = (f32[5,2,8,128]{3,2,1,0:T(8,128)S(1)}, f32[5,2,8,128]{3,2,1,0:T(8,128)}, u32[]{:S(2)}) copy-start(f32[5,2,8,128]{3,2,1,0:T(8,128)} %get-tuple-element.22.own_halo) | copy-start | bytes 122884
where the time goes:
time: 52.1 us; the launch traced here: 51.9 us
  Pallas kernels  33.4 us (64%)
  starting transfers between devices  13 us (25%)
  local copies, waits for them, and re-layouts  2.8 us (5%)
  waiting for transfers between devices  1.86 us (4%)
  between operations  0.77 us (1%)
    pallas_call x1, Pallas kernels, main_block(): pl.pallas_call(main_body, out_shape=[out] * 4, scratch_shapes=[pltpu.VMEM...  24.7 us
    ppermute x1, starting transfers between devices, on_device(): from_b = lax.ppermute(to_b, AXES, route_b)  7.63 us
    ppermute x1, starting transfers between devices, on_device(): lax.ppermute(to_w, 'lon', [((i + 1) % lons, i) for i in range(lons)])  3.93 us
    pallas_call x1, Pallas kernels, strips_and_merge(): pl.pallas_call(strips_body, out_shape=[out] * 4, scratch_shapes=[pltpu.VM...  3.51 us
    unnamed x22, local copies, waits for them, and re-layouts  2.8 us
    pallas_call x1, Pallas kernels, assemble(): pl.pallas_call(assemble_body, out_shape=[jax.ShapeDtypeStruct((5, LEVELS,...  2.32 us
    ppermute x1, waiting for transfers between devices, on_device(): from_b = lax.ppermute(to_b, AXES, route_b)  1.85 us
    pallas_call x1, Pallas kernels, pack_rows(): pl.pallas_call(functools.partial(pack_rows_body, 0), grid=(1,), in_specs=...  1.69 us
  transfers between devices with their start and end apart: 4, of which 1 were waited for; matrix products, arithmetic and copies ran while one was open for 0% of the time, Pallas kernels for 50%

commit v1 on v0

--- a/solution.py
+++ b/solution.py
@@ -18,7 +18,8 @@
 PSCALE = 0.15 / 0.08
 ASCALE = 0.0625 / 0.08
 DRAG = 0.05
-VMEM = 48 * 1024 * 1024
+VMEM = 24 * 1024 * 1024
+SMALL = 4 * 1024 * 1024
 
 
 def lane_roll(x, amount):
@@ -76,16 +77,27 @@
     return 0.1 + 0.3 * (row + 0.5) / total
 
 
-def pack_rows_body(count, *refs):
-    low, high, (to_a, to_b) = refs[:5], refs[5:10], refs[10:]
+def pack_rows_body(*refs):
+    fields, (to_a, to_b), (low, high, low_mask, high_mask, arrived) = refs[:5], refs[5:7], refs[7:]
     odd = lax.rem(lax.axis_index("lat"), 2) == 1
     upper = row_index() < 4
+    copies = []
     for f in range(5):
+        for n, (start, held, mask) in enumerate(((0, low, low_mask), (ROWS - 8, high, high_mask))):
+            source = fields[f].at[:, pl.ds(start, 8), :]
+            target = held.at[f] if f < 4 else mask
+            copies.append(pltpu.make_async_copy(source, target, arrived.at[2 * f + n]))
+    for copy in copies:
+        copy.start()
+    for f in range(5):
+        copies[2 * f].wait()
+        copies[2 * f + 1].wait()
         for m in range(LEVELS // 2):
-            b0, b1 = low[f][2 * m], low[f][2 * m + 1]
-            t0, t1 = high[f][2 * m], high[f][2 * m + 1]
-            if f == 4:
-                b0, b1, t0, t1 = (w.astype(jnp.float32) for w in (b0, b1, t0, t1))
+            if f < 4:
+                b0, b1, t0, t1 = low[f, 2 * m], low[f, 2 * m + 1], high[f, 2 * m], high[f, 2 * m + 1]
+            else:
+                b0, b1 = low_mask[2 * m].astype(jnp.float32), low_mask[2 * m + 1].astype(jnp.float32)
+                t0, t1 = high_mask[2 * m].astype(jnp.float32), high_mask[2 * m + 1].astype(jnp.float32)
             bottom = jnp.where(upper, b0, row_roll(b1, 4))
             top = jnp.where(upper, row_roll(t0, 4), t1)
             to_a[f, m] = jnp.where(odd, bottom, top)
@@ -93,17 +105,22 @@
 
 
 def pack_rows(fields):
-    lows = [pl.BlockSpec((LEVELS, 8, LANES), lambda i: (0, 0, 0)) for _ in fields]
-    highs = [pl.BlockSpec((LEVELS, 8, LANES), lambda i: (0, CHUNKS - 1, 0)) for _ in fields]
     out = jax.ShapeDtypeStruct((5, LEVELS // 2, 8, LANES), jnp.float32)
     return pl.pallas_call(
-        functools.partial(pack_rows_body, 0),
-        grid=(1,),
-        in_specs=lows + highs,
-        out_specs=[pl.BlockSpec(out.shape, lambda i: (0, 0, 0, 0))] * 2,
+        pack_rows_body,
+        in_specs=[pl.BlockSpec(memory_space=pltpu.HBM)] * 5,
+        out_specs=[pl.BlockSpec(memory_space=pltpu.VMEM)] * 2,
         out_shape=[out, out],
+        scratch_shapes=[
+            pltpu.VMEM((4, LEVELS, 8, LANES), jnp.float32),
+            pltpu.VMEM((4, LEVELS, 8, LANES), jnp.float32),
+            pltpu.VMEM((LEVELS, 8, LANES), jnp.int32),
+            pltpu.VMEM((LEVELS, 8, LANES), jnp.int32),
+            pltpu.SemaphoreType.DMA((10,)),
+        ],
+        compiler_params=pltpu.CompilerParams(vmem_limit_bytes=SMALL),
         name="pack_rows",
-    )(*fields, *fields)
+    )(*[pltpu.with_memory_space_constraint(field, pltpu.HBM) for field in fields])
 
 
 def strip_of(levels):
@@ -130,8 +147,7 @@
     return total
 
 
-def pack_columns_body(*refs):
-    fields, (strips, to_e, to_w) = refs[:5], refs[5:]
+def pack_columns(fields, strips, to_e, to_w):
     slots = {}
     for i in range(CHUNKS):
         rows = pl.ds(8 * i, 8)
@@ -149,24 +165,13 @@
         to_w[CHUNKS + j] = squeeze(slots[j], 20)
 
 
-def pack_columns(fields):
-    part = jax.ShapeDtypeStruct((CHUNKS + CHUNKS // 4, 8, LANES), jnp.float32)
-    return pl.pallas_call(
-        pack_columns_body,
-        out_shape=[jax.ShapeDtypeStruct((5, 2, ROWS, LANES), jnp.float32), part, part],
-        compiler_params=pltpu.CompilerParams(vmem_limit_bytes=VMEM),
-        cost_estimate=pl.CostEstimate(flops=20_000_000, bytes_accessed=2_000_000, transcendentals=0),
-        name="pack_columns",
-    )(*fields)
-
-
 def mirrored(x):
-    row, lane = row_index(), lane_index()
+    row = row_index()
     for bit in (1, 2):
         x = jnp.where((row & bit) == 0, row_roll(x, 8 - bit), row_roll(x, bit))
-    for bit in (1, 2, 4, 8, 16, 32):
-        x = jnp.where((lane & bit) == 0, lane_roll(x, -bit), lane_roll(x, bit))
-    return lane_roll(x, 64)
+    flat = x.reshape(-1, LANES)
+    back = LANES - 1 - lax.broadcasted_iota(jnp.int32, flat.shape, 1)
+    return jnp.take_along_axis(flat, back, axis=1).reshape(x.shape)
 
 
 def assemble_body(from_a, from_b, part_e, part_w, halo, strips, to_e, to_w):
@@ -174,27 +179,27 @@
     odd = lax.rem(lat, 2) == 1
     at_top = lat == lax.axis_size("lat") - 1
     upper = row_index() < 4
+    pairs = 5 * LEVELS // 2
+
+    def write(north, south):
+        even = jnp.where(upper, north, row_roll(south, 4))
+        other = jnp.where(upper, row_roll(north, 4), south)
+        for n in range(pairs):
+            f, m = divmod(n, LEVELS // 2)
+            halo[f, 2 * m] = even[n]
+            halo[f, 2 * m + 1] = other[n]
 
     @pl.when(at_top)
     def _():
-        for f in range(5):
-            for m in range(LEVELS // 2):
-                south = row_roll(from_a[f, m], 4)
-                north = mirrored(from_b[f, m])
-                if f in (2, 3):
-                    north = -north
-                halo[f, 2 * m] = jnp.where(upper, north, south)
-                halo[f, 2 * m + 1] = jnp.where(upper, row_roll(north, 4), row_roll(south, 4))
+        north = mirrored(from_b[...].reshape(pairs, 8, LANES))
+        flip = LEVELS // 2 * 2
+        north = jnp.concatenate([north[:flip], -north[flip : 2 * flip], north[2 * flip :]], axis=0)
+        write(north, from_a[...].reshape(pairs, 8, LANES))
 
     @pl.when(jnp.logical_not(at_top))
     def _():
-        for f in range(5):
-            for m in range(LEVELS // 2):
-                a, b = from_a[f, m], from_b[f, m]
-                north = jnp.where(odd, b, a)
-                south = row_roll(jnp.where(odd, a, b), 4)
-                halo[f, 2 * m] = jnp.where(upper, north, south)
-                halo[f, 2 * m + 1] = jnp.where(upper, row_roll(north, 4), row_roll(south, 4))
+        a, b = from_a[...].reshape(pairs, 8, LANES), from_b[...].reshape(pairs, 8, LANES)
+        write(jnp.where(odd, b, a), jnp.where(odd, a, b))
 
     tiles = []
     for f in range(5):
@@ -221,128 +226,173 @@
             whole,
             whole,
         ],
+        compiler_params=pltpu.CompilerParams(vmem_limit_bytes=SMALL),
         name="assemble",
     )(from_a, from_b, part_e, part_w)
 
 
-PADDED = ROWS + 16
-TALL = PADDED + 8
+def step_scratch(chunks):
+    rows = 8 * chunks
+    f32 = jnp.float32
+    return [
+        pltpu.VMEM((4, LEVELS, rows + 8, LANES), f32),
+        pltpu.VMEM((4, LEVELS, rows + 8, LANES), f32),
+        pltpu.VMEM((LEVELS, rows + 8, LANES), f32),
+        pltpu.VMEM((5, LEVELS, rows, LANES), f32),
+        pltpu.VMEM((5, LEVELS, rows + 8, LANES), f32),
+        pltpu.VMEM((LEVELS, rows, LANES), f32),
+        pltpu.VMEM((LEVELS, rows, LANES), f32),
+        pltpu.VMEM((LEVELS, rows + 8, LANES), f32),
+        pltpu.VMEM((rows, LANES), f32),
+    ]
+
+
+def run_substeps(chunks, state_a, state_b, press, shifted, past, face_e, face_n, wet, turn):
+    rows_all = 8 * chunks
+
+    def load_faces(k, _):
+        here = wet[k, 0:rows_all]
+        face_e[k] = FACE * (here * lane_roll(here, -1))
+        face_n[k] = FACE * (here * wet[k, 1 : rows_all + 1])
+        return 0
+
+    lax.fori_loop(0, LEVELS, load_faces, 0)
+
+    def shift(src):
+        base = jnp.zeros((rows_all, LANES), jnp.float32)
+        for k in range(LEVELS):
+            h = density_tenth(src[0, k, 0:rows_all], src[1, k, 0:rows_all], (k + 0.5) / LEVELS)
+            base = base + h
+            press[k, 0:rows_all] = base
+            for q in range(4):
+                shifted[q, k] = lane_roll(src[q, k, 0:rows_all], -1)
+            shifted[4, k] = lane_roll(base, -1)
+            base = base + h
+
+    def update(src, dst, i, _):
+        start = pl.multiple_of(8 * i, 8)
+        rows, after = pl.ds(start, 8), pl.ds(start + 1, 8)
+        f = turn[rows]
+        for k in range(LEVELS):
+            now = [src[q, k, rows] for q in range(4)]
+            p0 = press[k, rows]
+            ahead = [shifted[q, k, rows] for q in range(5)]
+            east = along_faces(face_e[k, rows], now, ahead[:4], 2, p0, ahead[4])
+            west = [None if n == 3 else lane_roll(east[n], 1) for n in range(5)]
+            nxt = [src[q, k, after] for q in range(4)]
+            north = along_faces(face_n[k, rows], now, nxt, 3, p0, press[k, after])
+            for n in (0, 1, 2, 4):
+                past[n, k, pl.ds(start + 8, 8)] = north[n]
+            south = [None if n == 3 else past[n, k, pl.ds(start + 7, 8)] for n in range(5)]
+            new = combine(now, wet[k, rows], f, east, west, north, south)
+            for q in range(4):
+                dst[q, k, rows] = new[q]
+        return 0
+
+    def two_steps(half, _):
+        shift(state_a)
+        lax.fori_loop(0, chunks, functools.partial(update, state_a, state_b), 0, unroll=True)
+        shift(state_b)
+        lax.fori_loop(0, chunks, functools.partial(update, state_b, state_a), 0, unroll=True)
+        return 0
+
+    lax.fori_loop(0, NSUB // 2, two_steps, 0)
 
 
 def main_body(*refs):
-    fields, halo, outs = refs[:5], refs[5], refs[6:10]
-    state, press, face_e, face_n, wet, past, turn = refs[10:]
+    fields, outs, packs, scratch = refs[:5], refs[5:9], refs[9:12], refs[12:]
+    state, wet, turn = scratch[0], scratch[-2], scratch[-1]
+    pack_columns(fields, *packs)
     lat = lax.axis_index("lat")
-    total = ROWS * lax.axis_size("lat")
-    turn[...] = coriolis_rows(lat * ROWS, total, (PADDED, LANES), -8)
+    turn[...] = coriolis_rows(lat * ROWS, ROWS * lax.axis_size("lat"), (ROWS, LANES), 0)
 
     def load_in(k, _):
         for f in range(4):
-            state[0, f, k, 0:8] = halo[f, k]
-            state[0, f, k, 8 : 8 + ROWS] = fields[f][k]
-            state[0, f, k, 8 + ROWS : PADDED] = halo[f, k]
-        wet[k, 0:8] = halo[4, k]
-        wet[k, 8 : 8 + ROWS] = fields[4][k].astype(jnp.float32)
-        wet[k, 8 + ROWS : PADDED] = halo[4, k]
+            state[f, k, 0:ROWS] = fields[f][k]
+        wet[k, 0:ROWS] = fields[4][k].astype(jnp.float32)
         return 0
 
     lax.fori_loop(0, LEVELS, load_in, 0)
-
-    def load_faces(k, _):
-        here = wet[k, 0:PADDED]
-        face_e[k] = FACE * (here * lane_roll(here, -1))
-        face_n[k] = FACE * (here * wet[k, 1 : PADDED + 1])
-        return 0
-
-    lax.fori_loop(0, LEVELS, load_faces, 0)
-
-    def pressure(src, i, _):
-        rows = pl.ds(pl.multiple_of(8 * i, 8), 8)
-        base = jnp.zeros((8, LANES), jnp.float32)
-        for k in range(LEVELS):
-            h = density_tenth(state[src, 0, k, rows], state[src, 1, k, rows], (k + 0.5) / LEVELS)
-            base = base + h
-            press[k, rows] = base
-            base = base + h
-        return 0
-
-    def northern(src, k, i, now, p0):
-        after = pl.ds(8 * i + 1, 8)
-        nxt = [state[src, f, k, after] for f in range(4)]
-        return along_faces(face_n[k, pl.ds(8 * i, 8)], now, nxt, 3, p0, press[k, after])
-
-    def update(src, store, i, _):
-        rows = pl.ds(8 * i, 8)
-        f = turn[rows]
-        for k in range(LEVELS):
-            now = [state[src, q, k, rows] for q in range(4)]
-            p0 = press[k, rows]
-            east = along_faces(
-                face_e[k, rows], now, [lane_roll(q, -1) for q in now], 2, p0, lane_roll(p0, -1)
-            )
-            west = [
-                lane_roll(east[0], 1),
-                lane_roll(east[1], 1),
-                lane_roll(east[2], 1),
-                None,
-                lane_roll(east[4], 1),
-            ]
-            north = northern(src, k, i, now, p0)
-            for n in (0, 1, 2, 4):
-                past[n, k, pl.ds(8 + 8 * i, 8)] = north[n]
-            south = [None if n == 3 else past[n, k, pl.ds(7 + 8 * i, 8)] for n in range(5)]
-            store(k, i, combine(now, wet[k, rows], f, east, west, north, south))
-        return 0
-
-    for step in range(NSUB):
-        src = step % 2
-        for i in range(CHUNKS + 2):
-            pressure(src, i, 0)
-        if step < NSUB - 1:
-
-            def store(k, i, new):
-                for q in range(4):
-                    state[1 - src, q, k, pl.ds(8 * i, 8)] = new[q]
-
-            for i in range(CHUNKS + 2):
-                update(src, store, i, 0)
-        else:
-
-            def store(k, i, new):
-                for q in range(4):
-                    outs[q][k, pl.ds(8 * (i - 1), 8)] = new[q]
-
-            for k in range(LEVELS):
-                now = [state[src, q, k, 0:8] for q in range(4)]
-                north = northern(src, k, 0, now, press[k, 0:8])
-                for n in (0, 1, 2, 4):
-                    past[n, k, 8:16] = north[n]
-            for i in range(1, CHUNKS + 1):
-                update(src, store, i, 0)
-
-
-def main_block(fields, halo):
+    run_substeps(CHUNKS, *scratch)
+
+    def store_out(k, _):
+        for f in range(4):
+            outs[f][k] = state[f, k, 0:ROWS]
+        return 0
+
+    lax.fori_loop(0, LEVELS, store_out, 0)
+
+
+def main_block(fields):
     out = jax.ShapeDtypeStruct((LEVELS, ROWS, LANES), jnp.float32)
-    f32 = jnp.float32
+    own = jax.ShapeDtypeStruct((5, 2, ROWS, LANES), jnp.float32)
+    part = jax.ShapeDtypeStruct((CHUNKS + CHUNKS // 4, 8, LANES), jnp.float32)
     return pl.pallas_call(
         main_body,
-        out_shape=[out] * 4,
-        scratch_shapes=[
-            pltpu.VMEM((2, 4, LEVELS, TALL, LANES), f32),
-            pltpu.VMEM((LEVELS, TALL, LANES), f32),
-            pltpu.VMEM((LEVELS, PADDED, LANES), f32),
-            pltpu.VMEM((LEVELS, PADDED, LANES), f32),
-            pltpu.VMEM((LEVELS, TALL, LANES), f32),
-            pltpu.VMEM((5, LEVELS, TALL, LANES), f32),
-            pltpu.VMEM((PADDED, LANES), f32),
-        ],
+        out_shape=[out] * 4 + [own, part, part],
+        scratch_shapes=step_scratch(CHUNKS),
         compiler_params=pltpu.CompilerParams(vmem_limit_bytes=VMEM),
         cost_estimate=pl.CostEstimate(flops=300_000_000, bytes_accessed=20_000_000, transcendentals=0),
         name="main_block",
-    )(*fields, halo)
-
-
-def strips_body(own, own_halo, from_w, from_e, *refs):
+    )(*fields)
+
+
+def bands_body(*refs):
+    low, high, halo, out, scratch = refs[:5], refs[5:10], refs[10], refs[11], refs[12:]
+    state, wet, turn = scratch[0], scratch[-2], scratch[-1]
+    lat = lax.axis_index("lat")
+    total = ROWS * lax.axis_size("lat")
+    turn[0:16] = coriolis_rows(lat * ROWS, total, (16, LANES), -8)
+    turn[16:32] = coriolis_rows(lat * ROWS, total, (16, LANES), ROWS - 8)
+
+    def load_in(k, _):
+        for f in range(4):
+            state[f, k, 0:8] = halo[f, k]
+            state[f, k, 8:16] = low[f][k]
+            state[f, k, 16:24] = high[f][k]
+            state[f, k, 24:32] = halo[f, k]
+        wet[k, 0:8] = halo[4, k]
+        wet[k, 8:16] = low[4][k].astype(jnp.float32)
+        wet[k, 16:24] = high[4][k].astype(jnp.float32)
+        wet[k, 24:32] = halo[4, k]
+        return 0
+
+    lax.fori_loop(0, LEVELS, load_in, 0)
+    run_substeps(4, *scratch)
+
+    def store_out(k, _):
+        for f in range(4):
+            out[f, k] = state[f, k, 8:24]
+        return 0
+
+    lax.fori_loop(0, LEVELS, store_out, 0)
+
+
+def edge_specs(fields):
+    low = [pl.BlockSpec((LEVELS, 8, LANES), lambda i: (0, 0, 0)) for _ in fields]
+    high = [pl.BlockSpec((LEVELS, 8, LANES), lambda i: (0, CHUNKS - 1, 0)) for _ in fields]
+    return low + high
+
+
+def bands(fields, halo):
+    out = jax.ShapeDtypeStruct((4, LEVELS, 16, LANES), jnp.float32)
+    return pl.pallas_call(
+        bands_body,
+        grid=(1,),
+        in_specs=edge_specs(fields) + [pl.BlockSpec(halo.shape, lambda i: (0, 0, 0, 0))],
+        out_specs=pl.BlockSpec(out.shape, lambda i: (0, 0, 0, 0)),
+        out_shape=out,
+        scratch_shapes=step_scratch(4),
+        compiler_params=pltpu.CompilerParams(vmem_limit_bytes=VMEM),
+        cost_estimate=pl.CostEstimate(flops=100_000_000, bytes_accessed=8_000_000, transcendentals=0),
+        name="bands",
+    )(*fields, *fields, halo)
+
+
+PADDED = ROWS + 16
+
+
+def strips_body(own, own_halo, from_w, from_e, band, *refs):
     mains, outs = refs[:4], refs[4:8]
     state, wet, turn = refs[8:]
     lat = lax.axis_index("lat")
@@ -409,17 +459,25 @@
 
     src = NSUB % 2
     lane = lane_index(ROWS)
+    upper = row_index() < 4
     for f in range(4):
         for k in range(LEVELS):
             tile = state[src, f, k // 4, 8 : 8 + ROWS]
             g = 32 * (k % 4)
-            block = mains[f][k]
+            block = jnp.concatenate(
+                [
+                    jnp.where(upper, band[f, k, 0:8], mains[f][k, 0:8]),
+                    mains[f][k, 8 : ROWS - 8],
+                    jnp.where(upper, mains[f][k, ROWS - 8 : ROWS], band[f, k, 8:16]),
+                ],
+                axis=0,
+            )
             block = jnp.where(lane < 4, lane_roll(tile, -(g + 20)), block)
             block = jnp.where(lane >= LANES - 4, lane_roll(tile, 124 - (g + 8)), block)
             outs[f][k] = block
 
 
-def strips_and_merge(own, own_halo, from_w, from_e, mains):
+def strips_and_merge(own, own_halo, from_w, from_e, band, mains):
     out = jax.ShapeDtypeStruct((LEVELS, ROWS, LANES), jnp.float32)
     f32 = jnp.float32
     return pl.pallas_call(
@@ -432,7 +490,7 @@
         ],
         compiler_params=pltpu.CompilerParams(vmem_limit_bytes=VMEM),
         name="strips_and_merge",
-    )(own, own_halo, from_w, from_e, *mains)
+    )(own, own_halo, from_w, from_e, band, *mains)
 
 
 def lat_routes(lats, lons):
@@ -453,12 +511,12 @@
     to_a, to_b = pack_rows(args)
     from_b = lax.ppermute(to_b, AXES, route_b)
     from_a = lax.ppermute(to_a, AXES, route_a)
-    own, part_e, part_w = pack_columns(args)
+    *mains, own, part_e, part_w = main_block(args)
     halo, own_halo, to_e, to_w = assemble(from_a, from_b, part_e, part_w)
     from_w = lax.ppermute(to_e, "lon", [(i, (i + 1) % lons) for i in range(lons)])
     from_e = lax.ppermute(to_w, "lon", [((i + 1) % lons, i) for i in range(lons)])
-    mains = main_block(args, halo)
-    return tuple(strips_and_merge(own, own_halo, from_w, from_e, mains))
+    band = bands(args, halo)
+    return tuple(strips_and_merge(own, own_halo, from_w, from_e, band, mains))
 
 
 def solution(mesh):

time: 52.1 us -> 27 us (0.52)
  Pallas kernels: 33.4 us -> 13.6 us
  local copies, waits for them, and re-layouts: 2.8 us -> 0.02 us
  waiting for transfers between devices: 1.86 us -> 0.01 us
    pallas_call x3, Pallas kernels: 27.6 us -> 9.83 us  [the longest x1 6.13 us: main_block(): pl.pallas_call(main_body, out_shape=[out] * 4 + [own, part, part], scratc...]
    unnamed x22 -> x10, local copies, waits for them, and re-layouts: 2.8 us -> 0.02 us
    pallas_call x1, Pallas kernels: 2.32 us -> 0.32 us  [assemble(): pl.pallas_call(assemble_body, out_shape=[jax.ShapeDtypeStruct((5, LEVELS,...]
    ppermute x1, waiting for transfers between devices: 1.85 us -> 0.01 us  [on_device(): from_b = lax.ppermute(to_b, AXES, route_b)]
    ppermute x1, starting transfers between devices: 3.93 us -> 2.9 us  [on_device(): lax.ppermute(to_w, 'lon', [((i + 1) % lons, i) for i in range(lons)])]
  transfers between devices with their start and end apart: 4 -> 4, of which waited for: 1 -> 0; matrix products, arithmetic and copies ran while one was open for 0% -> 0% of each run, Pallas kernels for 50% -> 32%
where the time goes in v1:
time: 27 us; the launch traced here: 26.9 us
  Pallas kernels  13.6 us (50%)
  starting transfers between devices  12.5 us (46%)
  between operations  0.78 us (3%)
    ppermute x1, starting transfers between devices, on_device(): from_b = lax.ppermute(to_b, AXES, route_b)  7.63 us
    pallas_call x1, Pallas kernels, main_block(): pl.pallas_call(main_body, out_shape=[out] * 4 + [own, part, part], scratc...  6.13 us
    pallas_call x1, Pallas kernels, strips_and_merge(): pl.pallas_call(strips_body, out_shape=[out] * 4, scratch_shapes=[pltpu.VM...  3.46 us
    ppermute x1, starting transfers between devices, on_device(): lax.ppermute(to_w, 'lon', [((i + 1) % lons, i) for i in range(lons)])  2.9 us
    pallas_call x1, Pallas kernels, bands(): pl.pallas_call(bands_body, grid=(1,), in_specs=edge_specs(fields) + [pl.B...  2.61 us
    pallas_call x1, Pallas kernels, pack_rows(): pl.pallas_call(pack_rows_body, in_specs=[pl.BlockSpec(memory_space=pltpu....  1.09 us
    ppermute x1, starting transfers between devices, on_device(): lax.ppermute(to_e, 'lon', [(i, (i + 1) % lons) for i in range(lons)])  1.02 us
    ppermute x1, starting transfers between devices, on_device(): from_a = lax.ppermute(to_a, AXES, route_a)  0.92 us
  transfers between devices with their start and end apart: 4, of which 0 were waited for; matrix products, arithmetic and copies ran while one was open for 0% of the time, Pallas kernels for 32%

profile of v1, /device:TPU:22, one launch (start us, length us, event | category | flops | bytes accessed | tf_op | source)
XLA Modules:
  0.0 26.9 jit_solution(16172807202247033062)
XLA Ops:
  0.6 0.0 copy-start.4
  0.6 0.0 copy-start.3
  0.7 0.0 copy-start.2
  0.7 0.0 copy-start.1
  0.7 0.0 copy-start
  0.7 1.1 %pack_rows.1 = (f32[5,4,8,128]{3,2,1,0:T(8,128)S(1)}, f32[5,4,8,128]{3,2,1,0:T(8,128)S(1)}) custom-call(f32[8,64,128]{2,1,0:T(8,128)} %refs_5_.1, f32[8,64,128]{2,1,0:T(8,128)} %refs_6_.1, f32[8,64,128]{2,1,0:T(8,128)} %refs_7_.1, f32[8,64,128]{2,1,0:T(8,128)} %refs_8_.1, s32[8,64,128]{2,1,0:T(8,128)} %refs_9_.1), custom_call_target="tpu_custom_call" | custom-call | tf_op jit(solution)/shard_map/pack_rows/pallas_call | solution.py:109
  1.8 0.9 %collective-permute-start = (f32[5,4,8,128]{3,2,1,0:T(8,128)S(1)}, f32[5,4,8,128]{3,2,1,0:T(8,128)S(1)}, u32[]{:S(2)}, u32[]{:S(2)}) collective-permute-start(f32[5,4,8,128]{3,2,1,0:T(8,128)S(1)} %get-tuple-element.18), channel_id=1, source_target_pairs={{0,32},{32,0},{64,96},{96,64},{128,160},{160,128},{192,224},{224,1... | collective-permute-start | bytes 245768 | tf_op jit(solution)/shard_map/ppermute | solution.py:513
  2.7 7.6 %collective-permute-start.1 = (f32[5,4,8,128]{3,2,1,0:T(8,128)S(1)}, f32[5,4,8,128]{3,2,1,0:T(8,128)S(1)}, u32[]{:S(2)}, u32[]{:S(2)}) collective-permute-start(f32[5,4,8,128]{3,2,1,0:T(8,128)S(1)} %get-tuple-element.19), channel_id=1, source_target_pairs={{32,64},{64,32},{96,128},{128,96},{160,192},{192,160},{224,255},{3... | collective-permute-start | bytes 245768 | tf_op jit(solution)/shard_map/ppermute | solution.py:512
  10.3 0.0 copy-done.4
  10.3 0.0 copy-done.3
  10.4 0.0 copy-done.2
  10.4 0.0 copy-done.1
  10.4 0.0 copy-done
  10.4 6.1 %main_block.1 = (f32[8,64,128]{2,1,0:T(8,128)S(1)}, f32[8,64,128]{2,1,0:T(8,128)S(1)}, f32[8,64,128]{2,1,0:T(8,128)S(1)}, f32[8,64,128]{2,1,0:T(8,128)S(1)}, f32...) custom-call(f32[8,64,128]{2,1,0:T(8,128)S(1)} %copy-done, ...), custom_call_target="tpu_custom_call" | custom-call | flops 300000000 | bytes 20000000 | tf_op jit(solution)/shard_map/main_block/pallas_call | solution.py:330
  16.5 0.0 collective-permute-done.from_a
  16.5 0.0 collective-permute-done.1.from_b
  16.5 0.3 %assemble.1 = (f32[5,8,8,128]{3,2,1,0:T(8,128)S(1)}, f32[5,2,8,128]{3,2,1,0:T(8,128)S(1)}, f32[12,8,128]{2,1,0:T(8,128)S(1)}, f32[12,8,128]{2,1,0:T(8,128)S(1)}) custom-call(f32[5,4,8,128]{3,2,1,0:T(8,128)S(1)} %collective-permute-done.from_a, f32[5,4,8,128]{3,2,1,0:T(8,128)S(1)} %collective-permute-done.1.from_b, ...), custom_call_target="tpu_custom_call" | custom-call | tf_op jit(solution)/shard_map/assemble/pallas_call | solution.py:221
  16.9 1.0 %collective-permute-start.2 = (f32[12,8,128]{2,1,0:T(8,128)S(1)}, f32[12,8,128]{2,1,0:T(8,128)S(1)}, u32[]{:S(2)}, u32[]{:S(2)}) collective-permute-start(f32[12,8,128]{2,1,0:T(8,128)S(1)} %get-tuple-element.23), channel_id=1, source_target_pairs={{0,1},{1,2},{2,3},{3,4},{4,5},{5,6},{6,7},{7,8},{8,9},{9,10},{10,1... | collective-permute-start | bytes 147464 | tf_op jit(solution)/shard_map/ppermute | solution.py:516
  17.9 2.9 %collective-permute-start.3 = (f32[12,8,128]{2,1,0:T(8,128)S(1)}, f32[12,8,128]{2,1,0:T(8,128)S(1)}, u32[]{:S(2)}, u32[]{:S(2)}) collective-permute-start(f32[12,8,128]{2,1,0:T(8,128)S(1)} %get-tuple-element.24), channel_id=1, source_target_pairs={{1,0},{2,1},{3,2},{4,3},{5,4},{6,5},{7,6},{8,7},{9,8},{10,9},{11,1... | collective-permute-start | bytes 147464 | tf_op jit(solution)/shard_map/ppermute | solution.py:517
  20.8 2.6 %bands.1.band = f32[4,8,16,128]{3,2,1,0:T(8,128)S(1)} custom-call(f32[8,64,128]{2,1,0:T(8,128)S(1)} %copy-done, f32[8,64,128]{2,1,0:T(8,128)S(1)} %copy-done.1, f32[8,64,128]{2,1,0:T(8,128)S(1)} %copy-done.2, f32[8,64,128]{2,1,0:T(8,128)S(1)} %copy-done.3, s32[8,64,128]{2,1,0:T(8,128)S(1)} %copy-done.4, f32[8,64,128]{2,1,0:T(8,128)S(1)} %copy-done, ...), custom_call_target="tpu_custom_call" | custom-call | flops 100000000 | bytes 8000000 | tf_op jit(solution)/shard_map/bands/pallas_call | solution.py:379
  23.4 0.0 collective-permute-done.2.from_w
  23.4 0.0 collective-permute-done.3.from_e
  23.4 3.5 %strips_and_merge.1 = (f32[8,64,128]{2,1,0:T(8,128)}, f32[8,64,128]{2,1,0:T(8,128)}, f32[8,64,128]{2,1,0:T(8,128)}, f32[8,64,128]{2,1,0:T(8,128)}) custom-call(f32[5,2,64,128]{3,2,1,0:T(8,128)S(1)} %get-tuple-element.17.own, f32[5,2,8,128]{3,2,1,0:T(8,128)S(1)} %get-tuple-element.22.own_halo, f32[12,8,128]{2,1,0:T(8,128)S(1)} %collective-permute-done.2.from_w, ...), custom_call_target="tpu_custom_call" | custom-call | tf_op jit(solution)/shard_map/strips_and_merge/pallas_call | solution.py:483
Async XLA Ops:
  0.6 9.7 %copy-start.4 = (s32[8,64,128]{2,1,0:T(8,128)S(1)}, s32[8,64,128]{2,1,0:T(8,128)}, u32[]{:S(2)}) copy-start(s32[8,64,128]{2,1,0:T(8,128)} %refs_9_.1) | copy-start | bytes 786436
  0.6 9.7 %copy-start.3 = (f32[8,64,128]{2,1,0:T(8,128)S(1)}, f32[8,64,128]{2,1,0:T(8,128)}, u32[]{:S(2)}) copy-start(f32[8,64,128]{2,1,0:T(8,128)} %refs_8_.1) | copy-start | bytes 786436
  0.7 9.7 %copy-start.2 = (f32[8,64,128]{2,1,0:T(8,128)S(1)}, f32[8,64,128]{2,1,0:T(8,128)}, u32[]{:S(2)}) copy-start(f32[8,64,128]{2,1,0:T(8,128)} %refs_7_.1) | copy-start | bytes 786436
  0.7 9.7 %copy-start.1 = (f32[8,64,128]{2,1,0:T(8,128)S(1)}, f32[8,64,128]{2,1,0:T(8,128)}, u32[]{:S(2)}) copy-start(f32[8,64,128]{2,1,0:T(8,128)} %refs_6_.1) | copy-start | bytes 786436
  0.7 9.7 %copy-start = (f32[8,64,128]{2,1,0:T(8,128)S(1)}, f32[8,64,128]{2,1,0:T(8,128)}, u32[]{:S(2)}) copy-start(f32[8,64,128]{2,1,0:T(8,128)} %refs_5_.1) | copy-start | bytes 786436
  1.8 14.7 %collective-permute-start = (f32[5,4,8,128]{3,2,1,0:T(8,128)S(1)}, f32[5,4,8,128]{3,2,1,0:T(8,128)S(1)}, u32[]{:S(2)}, u32[]{:S(2)}) collective-permute-start(f32[5,4,8,128]{3,2,1,0:T(8,128)S(1)} %get-tuple-element.18), channel_id=1, source_target_pairs={{0,32},{32,0},{64,96},{96,64},{128,160},{160,128},{192,224},{224,1... | collective-permute-start | bytes 245768 | tf_op jit(solution)/shard_map/ppermute | solution.py:513
  2.7 13.8 %collective-permute-start.1 = (f32[5,4,8,128]{3,2,1,0:T(8,128)S(1)}, f32[5,4,8,128]{3,2,1,0:T(8,128)S(1)}, u32[]{:S(2)}, u32[]{:S(2)}) collective-permute-start(f32[5,4,8,128]{3,2,1,0:T(8,128)S(1)} %get-tuple-element.19), channel_id=1, source_target_pairs={{32,64},{64,32},{96,128},{128,96},{160,192},{192,160},{224,255},{3... | collective-permute-start | bytes 245768 | tf_op jit(solution)/shard_map/ppermute | solution.py:512
  16.9 6.5 %collective-permute-start.2 = (f32[12,8,128]{2,1,0:T(8,128)S(1)}, f32[12,8,128]{2,1,0:T(8,128)S(1)}, u32[]{:S(2)}, u32[]{:S(2)}) collective-permute-start(f32[12,8,128]{2,1,0:T(8,128)S(1)} %get-tuple-element.23), channel_id=1, source_target_pairs={{0,1},{1,2},{2,3},{3,4},{4,5},{5,6},{6,7},{7,8},{8,9},{9,10},{10,1... | collective-permute-start | bytes 147464 | tf_op jit(solution)/shard_map/ppermute | solution.py:516
  17.9 5.5 %collective-permute-start.3 = (f32[12,8,128]{2,1,0:T(8,128)S(1)}, f32[12,8,128]{2,1,0:T(8,128)S(1)}, u32[]{:S(2)}, u32[]{:S(2)}) collective-permute-start(f32[12,8,128]{2,1,0:T(8,128)S(1)} %get-tuple-element.24), channel_id=1, source_target_pairs={{1,0},{2,1},{3,2},{4,3},{5,4},{6,5},{7,6},{8,7},{9,8},{10,9},{11,1... | collective-permute-start | bytes 147464 | tf_op jit(solution)/shard_map/ppermute | solution.py:517

commit v2 on v1

v2 whole, which is shorter than its diff:
```python
import functools

import jax
import jax.numpy as jnp
from jax import lax
from jax.experimental import pallas as pl
from jax.experimental.pallas import tpu as pltpu
from jax.sharding import PartitionSpec as P

NSUB = 4
LEVELS = 8
ROWS = 64
LANES = 128
CHUNKS = ROWS // 8
AXES = ("lat", "lon")

FACE = 0.08
ASCALE = 0.0625 / 0.08
PSCALE = ASCALE * 0.15 / 0.08
DRAG = 0.05
VMEM = 24 * 1024 * 1024
SMALL = 4 * 1024 * 1024


def lane_roll(x, amount):
    amount %= LANES
    return x if amount == 0 else pltpu.roll(x, amount, axis=x.ndim - 1)


def row_roll(x, amount):
    return pltpu.roll(x, amount, axis=x.ndim - 2)


def lane_index(rows=8):
    return lax.broadcasted_iota(jnp.int32, (rows, LANES), 1)


def row_index():
    return lax.broadcasted_iota(jnp.int32, (8, LANES), 0)


def density_tenth(temper, salt, depth):
    c = PSCALE * 0.1
    return salt * (c * 0.8 + (c * 0.03) * temper) - temper * (
        (c * 0.25 + c * 0.1 * depth) + (c * 0.06) * temper
    )


def along_faces(k, now, nxt, normal, press_now, press_nxt):
    t0, s0, t1, s1 = now[0], now[1], nxt[0], nxt[1]
    a = now[normal] + nxt[normal]
    less = k * (1.0 - a)
    more = k * (1.0 + a)
    ft = less * t1 - more * t0
    fs = less * s1 - more * s0
    dn = nxt[normal] - now[normal]
    dp = press_nxt - press_now
    tang = 5 - normal
    ftang = k * (nxt[tang] - now[tang])
    ahead = k * (dn - dp)
    behind = k * (dn + dp)
    return ft, fs, ftang, ahead, behind


def combine(now, keep, turn, east, west, north, south):
    t, s, u, v = now
    nt = t + ((east[0] - west[0]) + (north[0] - south[0]))
    ns = s + ((east[1] - west[1]) + (north[1] - south[1]))
    nu = (keep * u + turn * v) + ((east[3] - west[4]) + (north[2] - south[2]))
    nv = (keep * v - turn * u) + ((east[2] - west[2]) + (north[3] - south[4]))
    return nt, ns, nu, nv


def coriolis(row):
    total = ROWS * lax.axis_size("lat")
    row = row + lax.axis_index("lat") * ROWS
    row = jnp.where(row >= total, 2 * total - 1 - row, row).astype(jnp.float32)
    return 0.1 + 0.3 * (row + 0.5) / total


def pack_rows_body(*refs):
    fields, (to_b, to_a), (low, high, low_mask, high_mask, arrived) = refs[:5], refs[5:7], refs[7:]
    odd = lax.rem(lax.axis_index("lat"), 2) == 1
    upper = row_index() < 4
    copies = []
    for f in range(5):
        for n, (start, held, mask) in enumerate(((0, low, low_mask), (ROWS - 8, high, high_mask))):
            source = fields[f].at[:, pl.ds(start, 8), :]
            target = held.at[f] if f < 4 else mask
            copies.append(pltpu.make_async_copy(source, target, arrived.at[2 * f + n]))
    for copy in copies:
        copy.start()
    for f in range(5):
        copies[2 * f].wait()
        copies[2 * f + 1].wait()
        for m in range(LEVELS // 2):
            if f < 4:
                b0, b1, t0, t1 = low[f, 2 * m], low[f, 2 * m + 1], high[f, 2 * m], high[f, 2 * m + 1]
            else:
                b0, b1 = low_mask[2 * m].astype(jnp.float32), low_mask[2 * m + 1].astype(jnp.float32)
                t0, t1 = high_mask[2 * m].astype(jnp.float32), high_mask[2 * m + 1].astype(jnp.float32)
            bottom = jnp.where(upper, b0, row_roll(b1, 4))
            top = jnp.where(upper, row_roll(t0, 4), t1)
            to_a[f, m] = jnp.where(odd, bottom, top)
            to_b[f, m] = jnp.where(odd, top, bottom)


def pack_rows(fields):
    out = jax.ShapeDtypeStruct((5, LEVELS // 2, 8, LANES), jnp.float32)
    return pl.pallas_call(
        pack_rows_body,
        in_specs=[pl.BlockSpec(memory_space=pltpu.HBM)] * 5,
        out_specs=[pl.BlockSpec(memory_space=pltpu.VMEM)] * 2,
        out_shape=[out, out],
        scratch_shapes=[
            pltpu.VMEM((4, LEVELS, 8, LANES), jnp.float32),
            pltpu.VMEM((4, LEVELS, 8, LANES), jnp.float32),
            pltpu.VMEM((LEVELS, 8, LANES), jnp.int32),
            pltpu.VMEM((LEVELS, 8, LANES), jnp.int32),
            pltpu.SemaphoreType.DMA((10,)),
        ],
        compiler_params=pltpu.CompilerParams(vmem_limit_bytes=SMALL),
        name="pack_rows",
    )(*[pltpu.with_memory_space_constraint(field, pltpu.HBM) for field in fields])


def edge_tile(levels):
    lane = lane_index()
    total = lane_roll(levels[0], 8)
    for k in range(1, LEVELS):
        total = jnp.where(lane >= 16 * k, lane_roll(levels[k], 16 * k + 8), total)
    return total


def squeeze(tiles, start):
    place = lane_index() % 16
    total = lane_roll(tiles[0], -start)
    for n in range(1, len(tiles)):
        total = jnp.where(place >= 4 * n, lane_roll(tiles[n], 4 * n - start), total)
    return total


def send_to(odd, tiles):
    east, west = squeeze(tiles, 4), squeeze(tiles, 8)
    return jnp.where(odd, west, east), jnp.where(odd, east, west)


def odd_lon():
    return lax.rem(lax.axis_index("lon"), 2) == 1


def pack_columns(fields, edges, part_b, part_a):
    odd = odd_lon()
    tiles = []
    for i in range(CHUNKS):
        rows = pl.ds(8 * i, 8)
        tiles.append([edge_tile([fields[f][k, rows].astype(jnp.float32) for k in range(LEVELS)]) for f in range(5)])
    parts = [send_to(odd, row[:4]) for row in tiles]
    for j in range(CHUNKS // 4):
        parts.append(send_to(odd, [row[4] for row in tiles[4 * j : 4 * j + 4]]))
    for i, row in enumerate(tiles):
        for f in range(5):
            edges[f, 8 * i : 8 * i + 8] = row[f]
    for n, (to_a, to_b) in enumerate(parts):
        part_a[n] = to_a
        part_b[n] = to_b


def mirrored(x):
    row = row_index()
    for bit in (1, 2):
        x = jnp.where((row & bit) == 0, row_roll(x, 8 - bit), row_roll(x, bit))
    flat = x.reshape(-1, LANES)
    back = LANES - 1 - lax.broadcasted_iota(jnp.int32, flat.shape, 1)
    return jnp.take_along_axis(flat, back, axis=1).reshape(x.shape)


def assemble_body(from_b, from_a, part_b, part_a, halo, edges, to_b, to_a):
    lat = lax.axis_index("lat")
    odd = lax.rem(lat, 2) == 1
    at_top = lat == lax.axis_size("lat") - 1
    upper = row_index() < 4
    pairs = 5 * LEVELS // 2

    def write(north, south):
        even = jnp.where(upper, north, row_roll(south, 4))
        other = jnp.where(upper, row_roll(north, 4), south)
        for n in range(pairs):
            f, m = divmod(n, LEVELS // 2)
            halo[f, 2 * m] = even[n]
            halo[f, 2 * m + 1] = other[n]

    @pl.when(at_top)
    def _():
        north = mirrored(from_b[...].reshape(pairs, 8, LANES))
        flip = LEVELS // 2 * 2
        north = jnp.concatenate([north[:flip], -north[flip : 2 * flip], north[2 * flip :]], axis=0)
        write(north, from_a[...].reshape(pairs, 8, LANES))

    @pl.when(jnp.logical_not(at_top))
    def _():
        a, b = from_a[...].reshape(pairs, 8, LANES), from_b[...].reshape(pairs, 8, LANES)
        write(jnp.where(odd, b, a), jnp.where(odd, a, b))

    tiles = []
    for f in range(5):
        tile = edge_tile([halo[f, k] for k in range(LEVELS)])
        edges[f] = tile
        tiles.append(tile)
    for part, out in ((part_a, to_a), (part_b, to_b)):
        for i in range(CHUNKS):
            out[i] = part[i]
        for j in range(CHUNKS // 4):
            out[CHUNKS + 1 + j] = part[CHUNKS + j]
    last = CHUNKS + 1 + CHUNKS // 4
    to_a[CHUNKS], to_b[CHUNKS] = send_to(odd_lon(), tiles[:4])
    to_a[last], to_b[last] = send_to(odd_lon(), tiles[4:])


def assemble(from_b, from_a, part_b, part_a):
    whole = jax.ShapeDtypeStruct((CHUNKS + 2 + CHUNKS // 4, 8, LANES), jnp.float32)
    return pl.pallas_call(
        assemble_body,
        out_shape=[
            jax.ShapeDtypeStruct((5, LEVELS, 8, LANES), jnp.float32),
            jax.ShapeDtypeStruct((5, 8, LANES), jnp.float32),
            whole,
            whole,
        ],
        compiler_params=pltpu.CompilerParams(vmem_limit_bytes=SMALL),
        name="assemble",
    )(from_b, from_a, part_b, part_a)


def step_scratch(levels, chunks):
    rows = 8 * chunks
    f32 = jnp.float32
    return [
        pltpu.VMEM((4, levels, rows + 8, LANES), f32),
        pltpu.VMEM((4, levels, rows + 8, LANES), f32),
        pltpu.VMEM((levels, rows + 8, LANES), f32),
        pltpu.VMEM((5, levels, rows, LANES), f32),
        pltpu.VMEM((5, levels, rows + 8, LANES), f32),
        pltpu.VMEM((levels, rows, LANES), f32),
        pltpu.VMEM((levels, rows, LANES), f32),
        pltpu.VMEM((levels, rows, LANES), f32),
        pltpu.VMEM((levels, rows, LANES), f32),
        pltpu.VMEM((levels, rows + 8, LANES), f32),
    ]


def pressure_by_level(rows, src):
    base = jnp.zeros((rows, LANES), jnp.float32)
    for k in range(LEVELS):
        h = density_tenth(src[0, k, 0:rows], src[1, k, 0:rows], (k + 0.5) / LEVELS)
        base = base + h
        yield base
        base = base + h


def run_substeps(
    levels, chunks, pressure, turn_rows, state_a, state_b, press, shifted, past, face_e, face_n, keep, turn, wet
):
    rows_all = 8 * chunks

    def load_faces(k, _):
        here = wet[k, 0:rows_all]
        face_e[k] = FACE * (here * lane_roll(here, -1))
        face_n[k] = FACE * (here * wet[k, 1 : rows_all + 1])
        keep[k] = 1.0 - DRAG * here
        turn[k] = here * turn_rows
        return 0

    lax.fori_loop(0, levels, load_faces, 0, unroll=True)

    def shift(src):
        for k, base in enumerate(pressure(rows_all, src)):
            press[k, 0:rows_all] = base
            for q in range(4):
                shifted[q, k] = lane_roll(src[q, k, 0:rows_all], -1)
            shifted[4, k] = lane_roll(base, -1)

    def update(src, dst, i, _):
        start = pl.multiple_of(8 * i, 8)
        rows, after = pl.ds(start, 8), pl.ds(start + 1, 8)
        for k in range(levels):
            now = [src[q, k, rows] for q in range(4)]
            p0 = press[k, rows]
            ahead = [shifted[q, k, rows] for q in range(5)]
            east = along_faces(face_e[k, rows], now, ahead[:4], 2, p0, ahead[4])
            west = [None if n == 3 else lane_roll(east[n], 1) for n in range(5)]
            nxt = [src[q, k, after] for q in range(4)]
            north = along_faces(face_n[k, rows], now, nxt, 3, p0, press[k, after])
            for n in (0, 1, 2, 4):
                past[n, k, pl.ds(start + 8, 8)] = north[n]
            south = [None if n == 3 else past[n, k, pl.ds(start + 7, 8)] for n in range(5)]
            new = combine(now, keep[k, rows], turn[k, rows], east, west, north, south)
            for q in range(4):
                dst[q, k, rows] = new[q]
        return 0

    def two_steps(half, _):
        shift(state_a)
        lax.fori_loop(0, chunks, functools.partial(update, state_a, state_b), 0, unroll=True)
        shift(state_b)
        lax.fori_loop(0, chunks, functools.partial(update, state_b, state_a), 0, unroll=True)
        return 0

    lax.fori_loop(0, NSUB // 2, two_steps, 0)


def held(f, x):
    return x * ASCALE if f in (2, 3) else x


def given(f, x):
    return x * (1.0 / ASCALE) if f in (2, 3) else x


def main_body(*refs):
    fields, outs, packs, scratch = refs[:5], refs[5:9], refs[9:12], refs[12:]
    state, wet = scratch[0], scratch[-1]
    pack_columns(fields, *packs)

    def load_in(k, _):
        for f in range(4):
            state[f, k, 0:ROWS] = held(f, fields[f][k])
        wet[k, 0:ROWS] = fields[4][k].astype(jnp.float32)
        return 0

    lax.fori_loop(0, LEVELS, load_in, 0, unroll=True)
    turn_rows = coriolis(lax.broadcasted_iota(jnp.int32, (ROWS, LANES), 0))
    run_substeps(LEVELS, CHUNKS, pressure_by_level, turn_rows, *scratch)

    def store_out(k, _):
        for f in range(4):
            outs[f][k] = given(f, state[f, k, 0:ROWS])
        return 0

    lax.fori_loop(0, LEVELS, store_out, 0, unroll=True)


def main_block(fields):
    out = jax.ShapeDtypeStruct((LEVELS, ROWS, LANES), jnp.float32)
    edges = jax.ShapeDtypeStruct((5, ROWS, LANES), jnp.float32)
    part = jax.ShapeDtypeStruct((CHUNKS + CHUNKS // 4, 8, LANES), jnp.float32)
    return pl.pallas_call(
        main_body,
        out_shape=[out] * 4 + [edges, part, part],
        scratch_shapes=step_scratch(LEVELS, CHUNKS),
        compiler_params=pltpu.CompilerParams(vmem_limit_bytes=VMEM),
        cost_estimate=pl.CostEstimate(flops=300_000_000, bytes_accessed=20_000_000, transcendentals=0),
        name="main_block",
    )(*fields)


def bands_body(*refs):
    low, high, halo, out, scratch = refs[:5], refs[5:10], refs[10], refs[11], refs[12:]
    state, wet = scratch[0], scratch[-1]

    def load_in(k, _):
        for f in range(4):
            state[f, k, 0:8] = held(f, high[f][k])
            state[f, k, 8:16] = held(f, halo[f, k])
            state[f, k, 16:24] = held(f, low[f][k])
        wet[k, 0:8] = high[4][k].astype(jnp.float32)
        wet[k, 8:16] = halo[4, k]
        wet[k, 16:24] = low[4][k].astype(jnp.float32)
        return 0

    lax.fori_loop(0, LEVELS, load_in, 0, unroll=True)
    place = lax.broadcasted_iota(jnp.int32, (24, LANES), 0)
    turn_rows = coriolis(jnp.where(place < 12, place + (ROWS - 8), place - 16))
    run_substeps(LEVELS, 3, pressure_by_level, turn_rows, *scratch)

    def store_out(k, _):
        for f in range(4):
            out[f, k, 0:8] = given(f, state[f, k, 16:24])
            out[f, k, 8:16] = given(f, state[f, k, 0:8])
        return 0

    lax.fori_loop(0, LEVELS, store_out, 0, unroll=True)


def bands(fields, halo):
    low = [pl.BlockSpec((LEVELS, 8, LANES), lambda i: (0, 0, 0)) for _ in fields]
    high = [pl.BlockSpec((LEVELS, 8, LANES), lambda i: (0, CHUNKS - 1, 0)) for _ in fields]
    out = jax.ShapeDtypeStruct((4, LEVELS, 16, LANES), jnp.float32)
    return pl.pallas_call(
        bands_body,
        grid=(1,),
        in_specs=low + high + [pl.BlockSpec(halo.shape, lambda i: (0, 0, 0, 0))],
        out_specs=pl.BlockSpec(out.shape, lambda i: (0, 0, 0, 0)),
        out_shape=out,
        scratch_shapes=step_scratch(LEVELS, 3),
        compiler_params=pltpu.CompilerParams(vmem_limit_bytes=VMEM),
        cost_estimate=pl.CostEstimate(flops=100_000_000, bytes_accessed=8_000_000, transcendentals=0),
        name="bands",
    )(*fields, *fields, halo)


TALL = CHUNKS + 2


def pressure_by_lanes(rows, src):
    group = lax.broadcasted_iota(jnp.int32, (rows, LANES), 1) // 16
    depth = (group.astype(jnp.float32) + 0.5) / LEVELS
    for t in range(2):
        h = density_tenth(src[0, t, 0:rows], src[1, t, 0:rows], depth)
        below = [jnp.where(group >= n, lane_roll(h, 16 * n), 0.0) for n in range(1, LEVELS)]
        while len(below) > 1:
            below = [sum(below[n : n + 2]) for n in range(0, len(below), 2)]
        yield 2.0 * below[0] + h


def strips_body(edges, edge_halo, from_b, from_a, band, *refs):
    mains, outs, scratch = refs[:4], refs[4:8], refs[8:18]
    merged, sent = refs[18:]
    state, wet = scratch[0], scratch[-1]
    odd = odd_lon()
    lane = lane_index()
    place = lane % 16
    east_halo = (place >= 8) & (place < 12)
    west_halo = (place >= 4) & (place < 8)
    for i in range(CHUNKS + 1):
        for f in range(5):
            slot, chunk = (f, i) if f < 4 else (i % 4, CHUNKS + 1 + i // 4)
            own = edges[f, 8 * i : 8 * i + 8] if i < CHUNKS else edge_halo[f]
            a, b = from_a[chunk], from_b[chunk]
            east = jnp.where(east_halo, lane_roll(jnp.where(odd, b, a), 8 - 4 * slot), own)
            west = jnp.where(west_halo, lane_roll(jnp.where(odd, a, b), 4 - 4 * slot), own)
            for c in [1 + i] if i < CHUNKS else [0, CHUNKS + 1]:
                for t, tile in enumerate((east, west)):
                    if f < 4:
                        state[f, t, 8 * c : 8 * c + 8] = held(f, tile)
                    else:
                        wet[t, 8 * c : 8 * c + 8] = tile

    turn_rows = coriolis(lax.broadcasted_iota(jnp.int32, (8 * TALL, LANES), 0) - 8)
    run_substeps(2, TALL, pressure_by_lanes, turn_rows, *scratch)

    upper = row_index() < 4
    outer = (lane < 4) | (lane >= LANES - 4)
    copies = []
    for f in range(4):
        for i in range(CHUNKS):
            rows = pl.ds(8 * i, 8)
            c = 8 * (i + 1)
            edge = given(f, jnp.where(place < 8, state[f, 0, c : c + 8], state[f, 1, c : c + 8]))
            for k in range(LEVELS):
                block = mains[f][k, rows]
                if i == 0:
                    block = jnp.where(upper, band[f, k, 0:8], block)
                if i == CHUNKS - 1:
                    block = jnp.where(upper, block, band[f, k, 8:16])
                merged[f, k, rows] = jnp.where(outer, lane_roll(edge, -(16 * k + 8)), block)
        for n in range(2):
            half = pl.ds(n * LEVELS // 2, LEVELS // 2)
            copies.append(pltpu.make_async_copy(merged.at[f, half], outs[f].at[half], sent.at[2 * f + n]))
            copies[-1].start()
    for copy in copies:
        copy.wait()


def strips_and_merge(edges, edge_halo, from_b, from_a, band, mains):
    out = jax.ShapeDtypeStruct((LEVELS, ROWS, LANES), jnp.float32)
    return pl.pallas_call(
        strips_body,
        out_specs=[pl.BlockSpec(memory_space=pl.ANY)] * 4,
        out_shape=[out] * 4,
        scratch_shapes=step_scratch(2, TALL)
        + [pltpu.VMEM((4, LEVELS, ROWS, LANES), jnp.float32), pltpu.SemaphoreType.DMA((8,))],
        compiler_params=pltpu.CompilerParams(vmem_limit_bytes=VMEM),
        name="strips_and_merge",
    )(edges, edge_halo, from_b, from_a, band, *mains)


def lat_routes(lats, lons):
    first, second = [], []
    for j in range(lons):
        for i in range(lats):
            first.append((i * lons + j, (i ^ 1) * lons + j))
        for i in range(1, lats - 1):
            other = i + 1 if i % 2 else i - 1
            second.append((i * lons + j, other * lons + j))
        second.append(((lats - 1) * lons + j, (lats - 1) * lons + lons - 1 - j))
    return first, second


def lon_routes(lons):
    first = [(j, j ^ 1) for j in range(lons)]
    second = [(j, (j + 1 if j % 2 else j - 1) % lons) for j in range(lons)]
    return first, second


def on_device(*args):
    route_a, route_b = lat_routes(lax.axis_size("lat"), lax.axis_size("lon"))
    to_b, to_a = pack_rows(args)
    from_b = lax.ppermute(to_b, AXES, route_b)
    from_a = lax.ppermute(to_a, AXES, route_a)
    *mains, edges, part_b, part_a = main_block(args)
    halo, edge_halo, to_b, to_a = assemble(from_b, from_a, part_b, part_a)
    route_a, route_b = lon_routes(lax.axis_size("lon"))
    from_b = lax.ppermute(to_b, "lon", route_b)
    from_a = lax.ppermute(to_a, "lon", route_a)
    band = bands(args, halo)
    return tuple(strips_and_merge(edges, edge_halo, from_b, from_a, band, mains))


def solution(mesh):
    spec = P(None, "lat", "lon")
    return jax.shard_map(
        on_device,
        mesh=mesh,
        in_specs=(spec,) * 5,
        out_specs=(spec,) * 4,
        check_vma=False,
    )
```

time: 27 us -> 25.2 us (0.933)
  the two profiles are of different devices: /device:TPU:22 before, /device:TPU:20 now
where the time goes in v2:
time: 25.2 us; the launch traced here: 25.1 us
  starting transfers between devices  11.3 us (45%)
  Pallas kernels  11.1 us (44%)
  waiting for transfers between devices  1.9 us (8%)
  between operations  0.74 us (3%)
    ppermute x1, starting transfers between devices, on_device(): from_a = lax.ppermute(to_a, AXES, route_a)  6.76 us
    pallas_call x1, Pallas kernels, main_block(): pl.pallas_call(main_body, out_shape=[out] * 4 + [edges, part, part], scra...  4.64 us
    pallas_call x1, Pallas kernels, strips_and_merge(): pl.pallas_call(strips_body, out_specs=[pl.BlockSpec(memory_space=pl.ANY)]...  3.48 us
    ppermute x1, starting transfers between devices, on_device(): from_b = lax.ppermute(to_b, AXES, route_b)  2.44 us
    ppermute x1, starting transfers between devices, on_device(): from_a = lax.ppermute(to_a, 'lon', route_a)  2.01 us
    ppermute x1, waiting for transfers between devices, on_device(): from_b = lax.ppermute(to_b, 'lon', route_b)  1.89 us
    pallas_call x1, Pallas kernels, bands(): pl.pallas_call(bands_body, grid=(1,), in_specs=low + high + [pl.BlockSpec...  1.7 us
    pallas_call x1, Pallas kernels, pack_rows(): pl.pallas_call(pack_rows_body, in_specs=[pl.BlockSpec(memory_space=pltpu....  1.09 us
  transfers between devices with their start and end apart: 4, of which 1 were waited for; matrix products, arithmetic and copies ran while one was open for 0% of the time, Pallas kernels for 25%

profile of v2, /device:TPU:20, one launch (start us, length us, event | category | flops | bytes accessed | tf_op | source)
XLA Modules:
  0.0 25.1 jit_solution(14647449447999102135)
XLA Ops:
  0.6 0.0 copy-start.4
  0.6 0.0 copy-start.3
  0.7 0.0 copy-start.2
  0.7 0.0 copy-start.1
  0.7 0.0 copy-start
  0.7 1.1 %pack_rows.1 = (f32[5,4,8,128]{3,2,1,0:T(8,128)S(1)}, f32[5,4,8,128]{3,2,1,0:T(8,128)S(1)}) custom-call(f32[8,64,128]{2,1,0:T(8,128)} %refs_5_.1, f32[8,64,128]{2,1,0:T(8,128)} %refs_6_.1, f32[8,64,128]{2,1,0:T(8,128)} %refs_7_.1, f32[8,64,128]{2,1,0:T(8,128)} %refs_8_.1, s32[8,64,128]{2,1,0:T(8,128)} %refs_9_.1), custom_call_target="tpu_custom_call" | custom-call | tf_op jit(solution)/shard_map/pack_rows/pallas_call | solution.py:110
  1.8 2.4 %collective-permute-start = (f32[5,4,8,128]{3,2,1,0:T(8,128)S(1)}, f32[5,4,8,128]{3,2,1,0:T(8,128)S(1)}, u32[]{:S(2)}, u32[]{:S(2)}) collective-permute-start(f32[5,4,8,128]{3,2,1,0:T(8,128)S(1)} %get-tuple-element.18), channel_id=1, source_target_pairs={{32,64},{64,32},{96,128},{128,96},{160,192},{192,160},{224,255},{3... | collective-permute-start | bytes 245768 | tf_op jit(solution)/shard_map/ppermute | solution.py:499
  4.2 6.8 %collective-permute-start.1 = (f32[5,4,8,128]{3,2,1,0:T(8,128)S(1)}, f32[5,4,8,128]{3,2,1,0:T(8,128)S(1)}, u32[]{:S(2)}, u32[]{:S(2)}) collective-permute-start(f32[5,4,8,128]{3,2,1,0:T(8,128)S(1)} %get-tuple-element.19), channel_id=1, source_target_pairs={{0,32},{32,0},{64,96},{96,64},{128,160},{160,128},{192,224},{224,1... | collective-permute-start | bytes 245768 | tf_op jit(solution)/shard_map/ppermute | solution.py:500
  11.0 0.0 copy-done.4
  11.0 0.0 copy-done.3
  11.0 0.0 copy-done.2
  11.0 0.0 copy-done.1
  11.0 0.0 copy-done
  11.0 4.6 %main_block.1 = (f32[8,64,128]{2,1,0:T(8,128)S(1)}, f32[8,64,128]{2,1,0:T(8,128)S(1)}, f32[8,64,128]{2,1,0:T(8,128)S(1)}, f32[8,64,128]{2,1,0:T(8,128)S(1)}, f32...) custom-call(f32[8,64,128]{2,1,0:T(8,128)S(1)} %copy-done, ...), custom_call_target="tpu_custom_call" | custom-call | flops 300000000 | bytes 20000000 | tf_op jit(solution)/shard_map/main_block/pallas_call | solution.py:347
  15.7 0.0 collective-permute-done.from_b
  15.7 0.0 collective-permute-done.1.from_a
  15.7 0.2 assemble.1
  15.9 0.1 collective-permute-start.2
  16.0 2.0 %collective-permute-start.3 = (f32[12,8,128]{2,1,0:T(8,128)S(1)}, f32[12,8,128]{2,1,0:T(8,128)S(1)}, u32[]{:S(2)}, u32[]{:S(2)}) collective-permute-start(f32[12,8,128]{2,1,0:T(8,128)S(1)} %get-tuple-element.24), channel_id=1, source_target_pairs={{0,1},{1,0},{2,3},{3,2},{4,5},{5,4},{6,7},{7,6},{8,9},{9,8},{10,11... | collective-permute-start | bytes 147464 | tf_op jit(solution)/shard_map/ppermute | solution.py:505
  18.0 1.7 %bands.1.band = f32[4,8,16,128]{3,2,1,0:T(8,128)S(1)} custom-call(f32[8,64,128]{2,1,0:T(8,128)S(1)} %copy-done, f32[8,64,128]{2,1,0:T(8,128)S(1)} %copy-done.1, f32[8,64,128]{2,1,0:T(8,128)S(1)} %copy-done.2, f32[8,64,128]{2,1,0:T(8,128)S(1)} %copy-done.3, s32[8,64,128]{2,1,0:T(8,128)S(1)} %copy-done.4, f32[8,64,128]{2,1,0:T(8,128)S(1)} %copy-done, ...), custom_call_target="tpu_custom_call" | custom-call | flops 100000000 | bytes 8000000 | tf_op jit(solution)/shard_map/bands/pallas_call | solution.py:389
  19.7 1.9 %collective-permute-done.2.from_b = f32[12,8,128]{2,1,0:T(8,128)S(1)} collective-permute-done((f32[12,8,128]{2,1,0:T(8,128)S(1)}, f32[12,8,128]{2,1,0:T(8,128)S(1)}, u32[]{:S(2)}, u32[]{:S(2)}) %collective-permute-start.2) | collective-permute-done | bytes 49184 | tf_op jit(solution)/shard_map/ppermute | solution.py:504
  21.6 0.0 collective-permute-done.3.from_a
  21.6 3.5 %strips_and_merge.1 = (f32[8,64,128]{2,1,0:T(8,128)}, f32[8,64,128]{2,1,0:T(8,128)}, f32[8,64,128]{2,1,0:T(8,128)}, f32[8,64,128]{2,1,0:T(8,128)}) custom-call(f32[5,64,128]{2,1,0:T(8,128)S(1)} %get-tuple-element.17.edges, f32[5,8,128]{2,1,0:T(8,128)S(1)} %get-tuple-element.22.edge_halo, f32[12,8,128]{2,1,0:T(8,128)S(1)} %collective-permute-done.2.from_b, ...), custom_call_target="tpu_custom_call" | custom-call | tf_op jit(solution)/shard_map/strips_and_merge/pallas_call | solution.py:467
Async XLA Ops:
  0.6 10.4 %copy-start.4 = (s32[8,64,128]{2,1,0:T(8,128)S(1)}, s32[8,64,128]{2,1,0:T(8,128)}, u32[]{:S(2)}) copy-start(s32[8,64,128]{2,1,0:T(8,128)} %refs_9_.1) | copy-start | bytes 786436
  0.6 10.4 %copy-start.3 = (f32[8,64,128]{2,1,0:T(8,128)S(1)}, f32[8,64,128]{2,1,0:T(8,128)}, u32[]{:S(2)}) copy-start(f32[8,64,128]{2,1,0:T(8,128)} %refs_8_.1) | copy-start | bytes 786436
  0.7 10.4 %copy-start.2 = (f32[8,64,128]{2,1,0:T(8,128)S(1)}, f32[8,64,128]{2,1,0:T(8,128)}, u32[]{:S(2)}) copy-start(f32[8,64,128]{2,1,0:T(8,128)} %refs_7_.1) | copy-start | bytes 786436
  0.7 10.3 %copy-start.1 = (f32[8,64,128]{2,1,0:T(8,128)S(1)}, f32[8,64,128]{2,1,0:T(8,128)}, u32[]{:S(2)}) copy-start(f32[8,64,128]{2,1,0:T(8,128)} %refs_6_.1) | copy-start | bytes 786436
  0.7 10.3 %copy-start = (f32[8,64,128]{2,1,0:T(8,128)S(1)}, f32[8,64,128]{2,1,0:T(8,128)}, u32[]{:S(2)}) copy-start(f32[8,64,128]{2,1,0:T(8,128)} %refs_5_.1) | copy-start | bytes 786436
  1.8 13.9 %collective-permute-start = (f32[5,4,8,128]{3,2,1,0:T(8,128)S(1)}, f32[5,4,8,128]{3,2,1,0:T(8,128)S(1)}, u32[]{:S(2)}, u32[]{:S(2)}) collective-permute-start(f32[5,4,8,128]{3,2,1,0:T(8,128)S(1)} %get-tuple-element.18), channel_id=1, source_target_pairs={{32,64},{64,32},{96,128},{128,96},{160,192},{192,160},{224,255},{3... | collective-permute-start | bytes 245768 | tf_op jit(solution)/shard_map/ppermute | solution.py:499
  4.2 11.5 %collective-permute-start.1 = (f32[5,4,8,128]{3,2,1,0:T(8,128)S(1)}, f32[5,4,8,128]{3,2,1,0:T(8,128)S(1)}, u32[]{:S(2)}, u32[]{:S(2)}) collective-permute-start(f32[5,4,8,128]{3,2,1,0:T(8,128)S(1)} %get-tuple-element.19), channel_id=1, source_target_pairs={{0,32},{32,0},{64,96},{96,64},{128,160},{160,128},{192,224},{224,1... | collective-permute-start | bytes 245768 | tf_op jit(solution)/shard_map/ppermute | solution.py:500
  15.9 5.7 %collective-permute-start.2 = (f32[12,8,128]{2,1,0:T(8,128)S(1)}, f32[12,8,128]{2,1,0:T(8,128)S(1)}, u32[]{:S(2)}, u32[]{:S(2)}) collective-permute-start(f32[12,8,128]{2,1,0:T(8,128)S(1)} %get-tuple-element.23), channel_id=1, source_target_pairs={{0,31},{1,2},{2,1},{3,4},{4,3},{5,6},{6,5},{7,8},{8,7},{9,10},{10,... | collective-permute-start | bytes 147464 | tf_op jit(solution)/shard_map/ppermute | solution.py:504
  16.0 5.6 %collective-permute-start.3 = (f32[12,8,128]{2,1,0:T(8,128)S(1)}, f32[12,8,128]{2,1,0:T(8,128)S(1)}, u32[]{:S(2)}, u32[]{:S(2)}) collective-permute-start(f32[12,8,128]{2,1,0:T(8,128)S(1)} %get-tuple-element.24), channel_id=1, source_target_pairs={{0,1},{1,0},{2,3},{3,2},{4,5},{5,4},{6,7},{7,6},{8,9},{9,8},{10,11... | collective-permute-start | bytes 147464 | tf_op jit(solution)/shard_map/ppermute | solution.py:505

commit v3 on v2

--- a/solution.py
+++ b/solution.py
@@ -78,46 +78,46 @@
     return 0.1 + 0.3 * (row + 0.5) / total
 
 
+def pack_pairs(take, top, out):
+    upper = row_index() < 4
+    for f in range(5):
+        for m in range(LEVELS // 2):
+            first, second = take(f, 2 * m), take(f, 2 * m + 1)
+            lows = jnp.where(upper, first, row_roll(second, 4))
+            highs = jnp.where(upper, row_roll(first, 4), second)
+            out[f, m] = jnp.where(top, highs, lows)
+
+
+def odd_lat():
+    return lax.rem(lax.axis_index("lat"), 2) == 1
+
+
 def pack_rows_body(*refs):
-    fields, (to_b, to_a), (low, high, low_mask, high_mask, arrived) = refs[:5], refs[5:7], refs[7:]
-    odd = lax.rem(lax.axis_index("lat"), 2) == 1
-    upper = row_index() < 4
+    fields, out, (held_rows, held_mask, arrived) = refs[:5], refs[5], refs[6:]
+    start = pl.multiple_of(jnp.where(odd_lat(), ROWS - 8, 0), 8)
     copies = []
     for f in range(5):
-        for n, (start, held, mask) in enumerate(((0, low, low_mask), (ROWS - 8, high, high_mask))):
-            source = fields[f].at[:, pl.ds(start, 8), :]
-            target = held.at[f] if f < 4 else mask
-            copies.append(pltpu.make_async_copy(source, target, arrived.at[2 * f + n]))
+        target = held_rows.at[f] if f < 4 else held_mask
+        copies.append(pltpu.make_async_copy(fields[f].at[:, pl.ds(start, 8), :], target, arrived.at[f]))
     for copy in copies:
         copy.start()
-    for f in range(5):
-        copies[2 * f].wait()
-        copies[2 * f + 1].wait()
-        for m in range(LEVELS // 2):
-            if f < 4:
-                b0, b1, t0, t1 = low[f, 2 * m], low[f, 2 * m + 1], high[f, 2 * m], high[f, 2 * m + 1]
-            else:
-                b0, b1 = low_mask[2 * m].astype(jnp.float32), low_mask[2 * m + 1].astype(jnp.float32)
-                t0, t1 = high_mask[2 * m].astype(jnp.float32), high_mask[2 * m + 1].astype(jnp.float32)
-            bottom = jnp.where(upper, b0, row_roll(b1, 4))
-            top = jnp.where(upper, row_roll(t0, 4), t1)
-            to_a[f, m] = jnp.where(odd, bottom, top)
-            to_b[f, m] = jnp.where(odd, top, bottom)
+    for copy in copies:
+        copy.wait()
+    pack_pairs(
+        lambda f, k: held_rows[f, k] if f < 4 else held_mask[k].astype(jnp.float32), odd_lat(), out
+    )
 
 
 def pack_rows(fields):
-    out = jax.ShapeDtypeStruct((5, LEVELS // 2, 8, LANES), jnp.float32)
     return pl.pallas_call(
         pack_rows_body,
         in_specs=[pl.BlockSpec(memory_space=pltpu.HBM)] * 5,
-        out_specs=[pl.BlockSpec(memory_space=pltpu.VMEM)] * 2,
-        out_shape=[out, out],
+        out_specs=pl.BlockSpec(memory_space=pltpu.VMEM),
+        out_shape=jax.ShapeDtypeStruct((5, LEVELS // 2, 8, LANES), jnp.float32),
         scratch_shapes=[
             pltpu.VMEM((4, LEVELS, 8, LANES), jnp.float32),
-            pltpu.VMEM((4, LEVELS, 8, LANES), jnp.float32),
             pltpu.VMEM((LEVELS, 8, LANES), jnp.int32),
-            pltpu.VMEM((LEVELS, 8, LANES), jnp.int32),
-            pltpu.SemaphoreType.DMA((10,)),
+            pltpu.SemaphoreType.DMA((5,)),
         ],
         compiler_params=pltpu.CompilerParams(vmem_limit_bytes=SMALL),
         name="pack_rows",
@@ -132,16 +132,13 @@
     return total
 
 
-def squeeze(tiles, start):
+def send_to(odd, tiles):
     place = lane_index() % 16
-    total = lane_roll(tiles[0], -start)
+    rolled = [lane_roll(tile, 4 * n - 8) for n, tile in enumerate(tiles)]
+    west = east = rolled[0]
     for n in range(1, len(tiles)):
-        total = jnp.where(place >= 4 * n, lane_roll(tiles[n], 4 * n - start), total)
-    return total
-
-
-def send_to(odd, tiles):
-    east, west = squeeze(tiles, 4), squeeze(tiles, 8)
+        west = jnp.where(place >= 4 * n, rolled[n], west)
+        east = jnp.where((place >= 4 * n - 4) & (place < 12), rolled[n], east)
     return jnp.where(odd, west, east), jnp.where(odd, east, west)
 
 
@@ -149,7 +146,15 @@
     return lax.rem(lax.axis_index("lon"), 2) == 1
 
 
-def pack_columns(fields, edges, part_b, part_a):
+def main_slot():
+    lat, lats, half = lax.axis_index("lat"), lax.axis_size("lat"), lax.axis_size("lon") // 2
+    place = lax.rem(lax.axis_index("lon"), half)
+    far = (lat == lats // 2 - 1) | (lat == lats // 2) | (lat == lats - 1)
+    late = (place >= half - 2) & jnp.logical_not(far)
+    return jnp.where((lat == lats - 2) & (place < 6), 0, jnp.where(late, 2, 1))
+
+
+def pack_columns(fields, edges, part_b, part_a, rim):
     odd = odd_lon()
     tiles = []
     for i in range(CHUNKS):
@@ -164,6 +169,10 @@
     for n, (to_a, to_b) in enumerate(parts):
         part_a[n] = to_a
         part_b[n] = to_b
+    for f in range(5):
+        for k in range(LEVELS):
+            rim[f, k, 0:8] = fields[f][k, 0:8].astype(jnp.float32)
+            rim[f, k, 8:16] = fields[f][k, ROWS - 8 : ROWS].astype(jnp.float32)
 
 
 def mirrored(x):
@@ -175,7 +184,7 @@
     return jnp.take_along_axis(flat, back, axis=1).reshape(x.shape)
 
 
-def assemble_body(from_b, from_a, part_b, part_a, halo, edges, to_b, to_a):
+def assemble_body(from_b, from_a, part_b, part_a, _, halo, edges, to_b, to_a):
     lat = lax.axis_index("lat")
     odd = lax.rem(lat, 2) == 1
     at_top = lat == lax.axis_size("lat") - 1
@@ -217,7 +226,7 @@
     to_a[last], to_b[last] = send_to(odd_lon(), tiles[4:])
 
 
-def assemble(from_b, from_a, part_b, part_a):
+def assemble(from_b, from_a, part_b, part_a, after):
     whole = jax.ShapeDtypeStruct((CHUNKS + 2 + CHUNKS // 4, 8, LANES), jnp.float32)
     return pl.pallas_call(
         assemble_body,
@@ -229,7 +238,7 @@
         ],
         compiler_params=pltpu.CompilerParams(vmem_limit_bytes=SMALL),
         name="assemble",
-    )(from_b, from_a, part_b, part_a)
+    )(from_b, from_a, part_b, part_a, after)
 
 
 def step_scratch(levels, chunks):
@@ -254,7 +263,7 @@
     for k in range(LEVELS):
         h = density_tenth(src[0, k, 0:rows], src[1, k, 0:rows], (k + 0.5) / LEVELS)
         base = base + h
-        yield base
+        yield base, lane_roll(base, -1)
         base = base + h
 
 
@@ -274,11 +283,11 @@
     lax.fori_loop(0, levels, load_faces, 0, unroll=True)
 
     def shift(src):
-        for k, base in enumerate(pressure(rows_all, src)):
+        for k, (base, ahead) in enumerate(pressure(rows_all, src)):
             press[k, 0:rows_all] = base
             for q in range(4):
                 shifted[q, k] = lane_roll(src[q, k, 0:rows_all], -1)
-            shifted[4, k] = lane_roll(base, -1)
+            shifted[4, k] = ahead
 
     def update(src, dst, i, _):
         start = pl.multiple_of(8 * i, 8)
@@ -317,10 +326,8 @@
     return x * (1.0 / ASCALE) if f in (2, 3) else x
 
 
-def main_body(*refs):
-    fields, outs, packs, scratch = refs[:5], refs[5:9], refs[9:12], refs[12:]
+def run_main(fields, outs, scratch):
     state, wet = scratch[0], scratch[-1]
-    pack_columns(fields, *packs)
 
     def load_in(k, _):
         for f in range(4):
@@ -334,38 +341,23 @@
 
     def store_out(k, _):
         for f in range(4):
-            outs[f][k] = given(f, state[f, k, 0:ROWS])
+            outs[f, k] = given(f, state[f, k, 0:ROWS])
         return 0
 
     lax.fori_loop(0, LEVELS, store_out, 0, unroll=True)
 
 
-def main_block(fields):
-    out = jax.ShapeDtypeStruct((LEVELS, ROWS, LANES), jnp.float32)
-    edges = jax.ShapeDtypeStruct((5, ROWS, LANES), jnp.float32)
-    part = jax.ShapeDtypeStruct((CHUNKS + CHUNKS // 4, 8, LANES), jnp.float32)
-    return pl.pallas_call(
-        main_body,
-        out_shape=[out] * 4 + [edges, part, part],
-        scratch_shapes=step_scratch(LEVELS, CHUNKS),
-        compiler_params=pltpu.CompilerParams(vmem_limit_bytes=VMEM),
-        cost_estimate=pl.CostEstimate(flops=300_000_000, bytes_accessed=20_000_000, transcendentals=0),
-        name="main_block",
-    )(*fields)
-
-
-def bands_body(*refs):
-    low, high, halo, out, scratch = refs[:5], refs[5:10], refs[10], refs[11], refs[12:]
+def run_bands(rim, halo, out, scratch):
     state, wet = scratch[0], scratch[-1]
 
     def load_in(k, _):
         for f in range(4):
-            state[f, k, 0:8] = held(f, high[f][k])
+            state[f, k, 0:8] = held(f, rim[f, k, 8:16])
             state[f, k, 8:16] = held(f, halo[f, k])
-            state[f, k, 16:24] = held(f, low[f][k])
-        wet[k, 0:8] = high[4][k].astype(jnp.float32)
+            state[f, k, 16:24] = held(f, rim[f, k, 0:8])
+        wet[k, 0:8] = rim[4, k, 8:16]
         wet[k, 8:16] = halo[4, k]
-        wet[k, 16:24] = low[4][k].astype(jnp.float32)
+        wet[k, 16:24] = rim[4, k, 0:8]
         return 0
 
     lax.fori_loop(0, LEVELS, load_in, 0, unroll=True)
@@ -382,21 +374,80 @@
     lax.fori_loop(0, LEVELS, store_out, 0, unroll=True)
 
 
-def bands(fields, halo):
-    low = [pl.BlockSpec((LEVELS, 8, LANES), lambda i: (0, 0, 0)) for _ in fields]
-    high = [pl.BlockSpec((LEVELS, 8, LANES), lambda i: (0, CHUNKS - 1, 0)) for _ in fields]
-    out = jax.ShapeDtypeStruct((4, LEVELS, 16, LANES), jnp.float32)
+MAIN = jax.ShapeDtypeStruct((4, LEVELS, ROWS, LANES), jnp.float32)
+
+
+def first_body(*refs):
+    fields, (out, edges, part_b, part_a, rim, to_a), scratch = refs[:5], refs[5:11], refs[11:]
+    pack_columns(fields, edges, part_b, part_a, rim)
+    start = pl.multiple_of(jnp.where(odd_lat(), 0, 8), 8)
+    pack_pairs(lambda f, k: rim[f, k, pl.ds(start, 8)], jnp.logical_not(odd_lat()), to_a)
+
+    @pl.when(main_slot() == 0)
+    def _():
+        run_main(fields, out, scratch)
+
+
+def first_block(fields):
+    f32 = jnp.float32
+    part = jax.ShapeDtypeStruct((CHUNKS + CHUNKS // 4, 8, LANES), f32)
     return pl.pallas_call(
-        bands_body,
-        grid=(1,),
-        in_specs=low + high + [pl.BlockSpec(halo.shape, lambda i: (0, 0, 0, 0))],
-        out_specs=pl.BlockSpec(out.shape, lambda i: (0, 0, 0, 0)),
-        out_shape=out,
-        scratch_shapes=step_scratch(LEVELS, 3),
+        first_body,
+        out_shape=[
+            MAIN,
+            jax.ShapeDtypeStruct((5, ROWS, LANES), f32),
+            part,
+            part,
+            jax.ShapeDtypeStruct((5, LEVELS, 16, LANES), f32),
+            jax.ShapeDtypeStruct((5, LEVELS // 2, 8, LANES), f32),
+        ],
+        scratch_shapes=step_scratch(LEVELS, CHUNKS),
         compiler_params=pltpu.CompilerParams(vmem_limit_bytes=VMEM),
-        cost_estimate=pl.CostEstimate(flops=100_000_000, bytes_accessed=8_000_000, transcendentals=0),
-        name="bands",
-    )(*fields, *fields, halo)
+        cost_estimate=pl.CostEstimate(flops=300_000_000, bytes_accessed=20_000_000, transcendentals=0),
+        name="first_block",
+    )(*fields)
+
+
+def second_body(*refs):
+    fields, (out, done), scratch = refs[:5], refs[6:8], refs[8:]
+    done[...] = jnp.zeros_like(done)
+
+    @pl.when(main_slot() == 1)
+    def _():
+        run_main(fields, out, scratch)
+
+
+def second_block(fields, after):
+    return pl.pallas_call(
+        second_body,
+        out_shape=[MAIN, jax.ShapeDtypeStruct((8, LANES), jnp.float32)],
+        scratch_shapes=step_scratch(LEVELS, CHUNKS),
+        compiler_params=pltpu.CompilerParams(vmem_limit_bytes=VMEM),
+        cost_estimate=pl.CostEstimate(flops=300_000_000, bytes_accessed=20_000_000, transcendentals=0),
+        name="second_block",
+    )(*fields, after)
+
+
+def third_body(*refs):
+    fields, (rim, halo, out, band) = refs[:5], refs[5:9]
+    main_scratch, band_scratch = refs[9:19], refs[19:]
+
+    @pl.when(main_slot() == 2)
+    def _():
+        run_main(fields, out, main_scratch)
+
+    run_bands(rim, halo, band, band_scratch)
+
+
+def third_block(fields, rim, halo):
+    return pl.pallas_call(
+        third_body,
+        out_shape=[MAIN, jax.ShapeDtypeStruct((4, LEVELS, 16, LANES), jnp.float32)],
+        scratch_shapes=step_scratch(LEVELS, CHUNKS) + step_scratch(LEVELS, 3),
+        compiler_params=pltpu.CompilerParams(vmem_limit_bytes=VMEM),
+        cost_estimate=pl.CostEstimate(flops=200_000_000, bytes_accessed=10_000_000, transcendentals=0),
+        name="third_block",
+    )(*fields, rim, halo)
 
 
 TALL = CHUNKS + 2
@@ -405,17 +456,26 @@
 def pressure_by_lanes(rows, src):
     group = lax.broadcasted_iota(jnp.int32, (rows, LANES), 1) // 16
     depth = (group.astype(jnp.float32) + 0.5) / LEVELS
-    for t in range(2):
-        h = density_tenth(src[0, t, 0:rows], src[1, t, 0:rows], depth)
-        below = [jnp.where(group >= n, lane_roll(h, 16 * n), 0.0) for n in range(1, LEVELS)]
-        while len(below) > 1:
-            below = [sum(below[n : n + 2]) for n in range(0, len(below), 2)]
-        yield 2.0 * below[0] + h
+    source = lax.broadcasted_iota(jnp.int32, (LANES, 2 * LANES), 0)
+    target = lax.broadcasted_iota(jnp.int32, (LANES, 2 * LANES), 1)
+    target = jnp.where(target < LANES, target, (target - (LANES - 1)) % LANES)
+    same = (source % 16) == (target % 16)
+    weights = jnp.where(same & (source < target), 2.0, jnp.where(source == target, 1.0, 0.0))
+    both = jnp.concatenate([density_tenth(src[0, t, 0:rows], src[1, t, 0:rows], depth) for t in range(2)], axis=0)
+    pieces = []
+    for _ in range(3):
+        pieces.append(both.astype(jnp.bfloat16))
+        both = both - pieces[-1].astype(jnp.float32)
+    p = jnp.dot(jnp.concatenate(pieces, axis=0), weights.astype(jnp.bfloat16), preferred_element_type=jnp.float32)
+    p = (p[4 * rows :] + p[2 * rows : 4 * rows]) + p[: 2 * rows]
+    yield p[:rows, :LANES], p[:rows, LANES:]
+    yield p[rows:, :LANES], p[rows:, LANES:]
 
 
 def strips_body(edges, edge_halo, from_b, from_a, band, *refs):
-    mains, outs, scratch = refs[:4], refs[4:8], refs[8:18]
-    merged, sent = refs[18:]
+    mains, outs, scratch = refs[:3], refs[3:7], refs[7:17]
+    merged, sent = refs[17:]
+    slot_now = jnp.full((8, LANES), main_slot())
     state, wet = scratch[0], scratch[-1]
     odd = odd_lon()
     lane = lane_index()
@@ -428,7 +488,7 @@
             own = edges[f, 8 * i : 8 * i + 8] if i < CHUNKS else edge_halo[f]
             a, b = from_a[chunk], from_b[chunk]
             east = jnp.where(east_halo, lane_roll(jnp.where(odd, b, a), 8 - 4 * slot), own)
-            west = jnp.where(west_halo, lane_roll(jnp.where(odd, a, b), 4 - 4 * slot), own)
+            west = jnp.where(west_halo, lane_roll(jnp.where(odd, a, b), 8 - 4 * slot), own)
             for c in [1 + i] if i < CHUNKS else [0, CHUNKS + 1]:
                 for t, tile in enumerate((east, west)):
                     if f < 4:
@@ -448,7 +508,8 @@
             c = 8 * (i + 1)
             edge = given(f, jnp.where(place < 8, state[f, 0, c : c + 8], state[f, 1, c : c + 8]))
             for k in range(LEVELS):
-                block = mains[f][k, rows]
+                block = jnp.where(slot_now == 1, mains[1][f, k, rows], mains[2][f, k, rows])
+                block = jnp.where(slot_now == 0, mains[0][f, k, rows], block)
                 if i == 0:
                     block = jnp.where(upper, band[f, k, 0:8], block)
                 if i == CHUNKS - 1:
@@ -495,16 +556,16 @@
 
 def on_device(*args):
     route_a, route_b = lat_routes(lax.axis_size("lat"), lax.axis_size("lon"))
-    to_b, to_a = pack_rows(args)
-    from_b = lax.ppermute(to_b, AXES, route_b)
+    from_b = lax.ppermute(pack_rows(args), AXES, route_b)
+    main_0, edges, part_b, part_a, rim, to_a = first_block(args)
     from_a = lax.ppermute(to_a, AXES, route_a)
-    *mains, edges, part_b, part_a = main_block(args)
-    halo, edge_halo, to_b, to_a = assemble(from_b, from_a, part_b, part_a)
+    main_1, done = second_block(args, edges)
+    halo, edge_halo, to_b, to_a = assemble(from_b, from_a, part_b, part_a, done)
     route_a, route_b = lon_routes(lax.axis_size("lon"))
     from_b = lax.ppermute(to_b, "lon", route_b)
     from_a = lax.ppermute(to_a, "lon", route_a)
-    band = bands(args, halo)
-    return tuple(strips_and_merge(edges, edge_halo, from_b, from_a, band, mains))
+    main_2, band = third_block(args, rim, halo)
+    return tuple(strips_and_merge(edges, edge_halo, from_b, from_a, band, (main_0, main_1, main_2)))
 
 
 def solution(mesh):

time: 25.2 us -> 23.9 us (0.948)
  the two profiles are of different devices: /device:TPU:20 before, /device:TPU:22 now
where the time goes in v3:
time: 23.9 us; the launch traced here: 23.8 us
  starting transfers between devices  11.3 us (47%)
  Pallas kernels  10.4 us (44%)
  waiting for transfers between devices  1.38 us (6%)
  between operations  0.77 us (3%)
    ppermute x1, starting transfers between devices, on_device(): from_b = lax.ppermute(pack_rows(args), AXES, route_b)  7.92 us
    pallas_call x1, Pallas kernels, second_block(): pl.pallas_call(second_body, out_shape=[MAIN, jax.ShapeDtypeStruct((8, LAN...  4.33 us
    ppermute x1, starting transfers between devices, on_device(): from_b = lax.ppermute(to_b, 'lon', route_b)  3.25 us
    pallas_call x1, Pallas kernels, strips_and_merge(): pl.pallas_call(strips_body, out_specs=[pl.BlockSpec(memory_space=pl.ANY)]...  2.63 us
    pallas_call x1, Pallas kernels, third_block(): pl.pallas_call(third_body, out_shape=[MAIN, jax.ShapeDtypeStruct((4, LEVE...  1.69 us
    pallas_call x1, Pallas kernels, pack_rows(): pl.pallas_call(pack_rows_body, in_specs=[pl.BlockSpec(memory_space=pltpu....  0.99 us
    ppermute x1, waiting for transfers between devices, on_device(): from_b = lax.ppermute(to_b, 'lon', route_b)  0.72 us
    ppermute x1, waiting for transfers between devices, on_device(): from_a = lax.ppermute(to_a, AXES, route_a)  0.66 us
  transfers between devices with their start and end apart: 4, of which 2 were waited for; matrix products, arithmetic and copies ran while one was open for 0% of the time, Pallas kernels for 27%

profile of v3, /device:TPU:22, one launch (start us, length us, event | category | flops | bytes accessed | tf_op | source)
XLA Modules:
  0.0 23.8 jit_solution(5461635159426232315)
XLA Ops:
  0.6 0.0 copy-start.4
  0.6 0.0 copy-start.3
  0.7 0.0 copy-start.2
  0.7 0.0 copy-start.1
  0.7 0.0 copy-start
  0.7 1.0 %pack_rows.1 = f32[5,4,8,128]{3,2,1,0:T(8,128)S(1)} custom-call(f32[8,64,128]{2,1,0:T(8,128)} %refs_0_.7, f32[8,64,128]{2,1,0:T(8,128)} %refs_1_.7, f32[8,64,128]{2,1,0:T(8,128)} %refs_2_.7, f32[8,64,128]{2,1,0:T(8,128)} %refs_3_.7, s32[8,64,128]{2,1,0:T(8,128)} %refs_4_.7), custom_call_target="tpu_custom_call" | custom-call | tf_op jit(solution)/shard_map/pack_rows/pallas_call | solution.py:112
  1.7 7.9 %collective-permute-start = (f32[5,4,8,128]{3,2,1,0:T(8,128)S(1)}, f32[5,4,8,128]{3,2,1,0:T(8,128)S(1)}, u32[]{:S(2)}, u32[]{:S(2)}) collective-permute-start(f32[5,4,8,128]{3,2,1,0:T(8,128)S(1)} %pack_rows.1), channel_id=1, source_target_pairs={{32,64},{64,32},{96,128},{128,96},{160,192},{192,160},{224,255},{3... | collective-permute-start | bytes 245768 | tf_op jit(solution)/shard_map/ppermute | solution.py:559
  9.6 0.0 copy-done.4
  9.6 0.0 copy-done.3
  9.6 0.0 copy-done.2
  9.6 0.0 copy-done.1
  9.6 0.0 copy-done
  9.7 0.5 %first_block.1 = (f32[4,8,64,128]{3,2,1,0:T(8,128)S(1)}, f32[5,64,128]{2,1,0:T(8,128)S(1)}, f32[10,8,128]{2,1,0:T(8,128)S(1)}, f32[10,8,128]{2,1,0:T(8,128)S(1)}...) custom-call(f32[8,64,128]{2,1,0:T(8,128)S(1)} %copy-done, f32[8,64,128]{2,1,0:T(8,128)S(1)} %copy-done.1, ...), custom_call_target="tpu_custom_call" | custom-call | flops 300000000 | bytes 20000000 | tf_op jit(solution)/shard_map/first_block/pallas_call | solution.py:394
  10.1 0.1 collective-permute-start.1
  10.2 4.3 %second_block.1 = (f32[4,8,64,128]{3,2,1,0:T(8,128)S(1)}, f32[8,128]{1,0:T(8,128)S(1)}) custom-call(f32[8,64,128]{2,1,0:T(8,128)S(1)} %copy-done, f32[8,64,128]{2,1,0:T(8,128)S(1)} %copy-done.1, f32[8,64,128]{2,1,0:T(8,128)S(1)} %copy-done.2, f32[8,64,128]{2,1,0:T(8,128)S(1)} %copy-done.3, s32[8,64,128]{2,1,0:T(8,128)S(1)} %copy-done.4, ...), custom_call_target="tpu_custom_call" | custom-call | flops 300000000 | bytes 20000000 | tf_op jit(solution)/shard_map/second_block/pallas_call | solution.py:421
  14.6 0.0 collective-permute-done.from_b
  14.6 0.7 %collective-permute-done.1.from_a = f32[5,4,8,128]{3,2,1,0:T(8,128)S(1)} collective-permute-done((f32[5,4,8,128]{3,2,1,0:T(8,128)S(1)}, f32[5,4,8,128]{3,2,1,0:T(8,128)S(1)}, u32[]{:S(2)}, u32[]{:S(2)}) %collective-permute-start.1) | collective-permute-done | bytes 81952 | tf_op jit(solution)/shard_map/ppermute | solution.py:561
  15.3 0.3 %assemble.1 = (f32[5,8,8,128]{3,2,1,0:T(8,128)S(1)}, f32[5,8,128]{2,1,0:T(8,128)S(1)}, f32[12,8,128]{2,1,0:T(8,128)S(1)}, f32[12,8,128]{2,1,0:T(8,128)S(1)}) custom-call(f32[5,4,8,128]{3,2,1,0:T(8,128)S(1)} %collective-permute-done.from_b, f32[5,4,8,128]{3,2,1,0:T(8,128)S(1)} %collective-permute-done.1.from_a, f32[10,8,128]{2,1,0:T(8,128)S(1)} %get-tuple-element.20.part_b, ...), custom_call_target="tpu_custom_call" | custom-call | tf_op jit(solution)/shard_map/assemble/pallas_call | solution.py:231
  15.5 3.2 %collective-permute-start.2 = (f32[12,8,128]{2,1,0:T(8,128)S(1)}, f32[12,8,128]{2,1,0:T(8,128)S(1)}, u32[]{:S(2)}, u32[]{:S(2)}) collective-permute-start(f32[12,8,128]{2,1,0:T(8,128)S(1)} %get-tuple-element.24), channel_id=1, source_target_pairs={{0,31},{1,2},{2,1},{3,4},{4,3},{5,6},{6,5},{7,8},{8,7},{9,10},{10,... | collective-permute-start | bytes 147464 | tf_op jit(solution)/shard_map/ppermute | solution.py:565
  18.8 0.0 collective-permute-start.3
  18.8 1.7 %third_block.1 = (f32[4,8,64,128]{3,2,1,0:T(8,128)S(1)}, f32[4,8,16,128]{3,2,1,0:T(8,128)S(1)}) custom-call(f32[8,64,128]{2,1,0:T(8,128)S(1)} %copy-done, f32[8,64,128]{2,1,0:T(8,128)S(1)} %copy-done.1, f32[8,64,128]{2,1,0:T(8,128)S(1)} %copy-done.2, f32[8,64,128]{2,1,0:T(8,128)S(1)} %copy-done.3, s32[8,64,128]{2,1,0:T(8,128)S(1)} %copy-done.4, ...), custom_call_target="tpu_custom_call" | custom-call | flops 200000000 | bytes 10000000 | tf_op jit(solution)/shard_map/third_block/pallas_call | solution.py:443
  20.5 0.7 %collective-permute-done.2.from_b = f32[12,8,128]{2,1,0:T(8,128)S(1)} collective-permute-done((f32[12,8,128]{2,1,0:T(8,128)S(1)}, f32[12,8,128]{2,1,0:T(8,128)S(1)}, u32[]{:S(2)}, u32[]{:S(2)}) %collective-permute-start.2) | collective-permute-done | bytes 49184 | tf_op jit(solution)/shard_map/ppermute | solution.py:565
  21.2 0.0 collective-permute-done.3.from_a
  21.2 2.6 %strips_and_merge.1 = (f32[8,64,128]{2,1,0:T(8,128)}, f32[8,64,128]{2,1,0:T(8,128)}, f32[8,64,128]{2,1,0:T(8,128)}, f32[8,64,128]{2,1,0:T(8,128)}) custom-call(f32[5,64,128]{2,1,0:T(8,128)S(1)} %get-tuple-element.18.refs_5_.edges, f32[5,8,128]{2,1,0:T(8,128)S(1)} %get-tuple-element.23.edge_halo, f32[12,8,128]{2,1,0:T(8,128)S(1)} %collective-permute-done.2.from_b, ...), custom_call_target="tpu_custom_call" | custom-call | tf_op jit(solution)/shard_map/strips_and_merge/pallas_call | solution.py:528
Async XLA Ops:
  0.6 9.0 %copy-start.4 = (s32[8,64,128]{2,1,0:T(8,128)S(1)}, s32[8,64,128]{2,1,0:T(8,128)}, u32[]{:S(2)}) copy-start(s32[8,64,128]{2,1,0:T(8,128)} %refs_4_.7) | copy-start | bytes 786436
  0.6 9.0 %copy-start.3 = (f32[8,64,128]{2,1,0:T(8,128)S(1)}, f32[8,64,128]{2,1,0:T(8,128)}, u32[]{:S(2)}) copy-start(f32[8,64,128]{2,1,0:T(8,128)} %refs_3_.7) | copy-start | bytes 786436
  0.7 9.0 %copy-start.2 = (f32[8,64,128]{2,1,0:T(8,128)S(1)}, f32[8,64,128]{2,1,0:T(8,128)}, u32[]{:S(2)}) copy-start(f32[8,64,128]{2,1,0:T(8,128)} %refs_2_.7) | copy-start | bytes 786436
  0.7 9.0 %copy-start.1 = (f32[8,64,128]{2,1,0:T(8,128)S(1)}, f32[8,64,128]{2,1,0:T(8,128)}, u32[]{:S(2)}) copy-start(f32[8,64,128]{2,1,0:T(8,128)} %refs_1_.7) | copy-start | bytes 786436
  0.7 9.0 %copy-start = (f32[8,64,128]{2,1,0:T(8,128)S(1)}, f32[8,64,128]{2,1,0:T(8,128)}, u32[]{:S(2)}) copy-start(f32[8,64,128]{2,1,0:T(8,128)} %refs_0_.7) | copy-start | bytes 786436
  1.7 12.9 %collective-permute-start = (f32[5,4,8,128]{3,2,1,0:T(8,128)S(1)}, f32[5,4,8,128]{3,2,1,0:T(8,128)S(1)}, u32[]{:S(2)}, u32[]{:S(2)}) collective-permute-start(f32[5,4,8,128]{3,2,1,0:T(8,128)S(1)} %pack_rows.1), channel_id=1, source_target_pairs={{32,64},{64,32},{96,128},{128,96},{160,192},{192,160},{224,255},{3... | collective-permute-start | bytes 245768 | tf_op jit(solution)/shard_map/ppermute | solution.py:559
  10.1 5.1 %collective-permute-start.1 = (f32[5,4,8,128]{3,2,1,0:T(8,128)S(1)}, f32[5,4,8,128]{3,2,1,0:T(8,128)S(1)}, u32[]{:S(2)}, u32[]{:S(2)}) collective-permute-start(f32[5,4,8,128]{3,2,1,0:T(8,128)S(1)} %get-tuple-element.19), channel_id=1, source_target_pairs={{0,32},{32,0},{64,96},{96,64},{128,160},{160,128},{192,224},{224,1... | collective-permute-start | bytes 245768 | tf_op jit(solution)/shard_map/ppermute | solution.py:561
  15.5 5.7 %collective-permute-start.2 = (f32[12,8,128]{2,1,0:T(8,128)S(1)}, f32[12,8,128]{2,1,0:T(8,128)S(1)}, u32[]{:S(2)}, u32[]{:S(2)}) collective-permute-start(f32[12,8,128]{2,1,0:T(8,128)S(1)} %get-tuple-element.24), channel_id=1, source_target_pairs={{0,31},{1,2},{2,1},{3,4},{4,3},{5,6},{6,5},{7,8},{8,7},{9,10},{10,... | collective-permute-start | bytes 147464 | tf_op jit(solution)/shard_map/ppermute | solution.py:565
  18.8 2.4 %collective-permute-start.3 = (f32[12,8,128]{2,1,0:T(8,128)S(1)}, f32[12,8,128]{2,1,0:T(8,128)S(1)}, u32[]{:S(2)}, u32[]{:S(2)}) collective-permute-start(f32[12,8,128]{2,1,0:T(8,128)S(1)} %get-tuple-element.25), channel_id=1, source_target_pairs={{0,1},{1,0},{2,3},{3,2},{4,5},{5,4},{6,7},{7,6},{8,9},{9,8},{10,11... | collective-permute-start | bytes 147464 | tf_op jit(solution)/shard_map/ppermute | solution.py:566

commit v4 on v3

--- a/solution.py
+++ b/solution.py
@@ -289,8 +289,10 @@
                 shifted[q, k] = lane_roll(src[q, k, 0:rows_all], -1)
             shifted[4, k] = ahead
 
-    def update(src, dst, i, _):
-        start = pl.multiple_of(8 * i, 8)
+    first_row = row_index() == 0
+
+    def update(src, dst, i, _, before=None):
+        start = 8 * i if isinstance(i, int) else pl.multiple_of(8 * i, 8)
         rows, after = pl.ds(start, 8), pl.ds(start + 1, 8)
         for k in range(levels):
             now = [src[q, k, rows] for q in range(4)]
@@ -300,9 +302,15 @@
             west = [None if n == 3 else lane_roll(east[n], 1) for n in range(5)]
             nxt = [src[q, k, after] for q in range(4)]
             north = along_faces(face_n[k, rows], now, nxt, 3, p0, press[k, after])
-            for n in (0, 1, 2, 4):
-                past[n, k, pl.ds(start + 8, 8)] = north[n]
-            south = [None if n == 3 else past[n, k, pl.ds(start + 7, 8)] for n in range(5)]
+            if before is None:
+                for n in (0, 1, 2, 4):
+                    past[n, k, pl.ds(start + 8, 8)] = north[n]
+                south = [None if n == 3 else past[n, k, pl.ds(start + 7, 8)] for n in range(5)]
+            else:
+                moved = [None if n == 3 else row_roll(north[n], 1) for n in range(5)]
+                held_over = before.get(k, moved)
+                south = [None if n == 3 else jnp.where(first_row, held_over[n], moved[n]) for n in range(5)]
+                before[k] = moved
             new = combine(now, keep[k, rows], turn[k, rows], east, west, north, south)
             for q in range(4):
                 dst[q, k, rows] = new[q]
@@ -310,9 +318,19 @@
 
     def two_steps(half, _):
         shift(state_a)
-        lax.fori_loop(0, chunks, functools.partial(update, state_a, state_b), 0, unroll=True)
+        if levels == 2:
+            before = {}
+            for i in range(chunks):
+                update(state_a, state_b, i, 0, before)
+        else:
+            lax.fori_loop(0, chunks, functools.partial(update, state_a, state_b), 0, unroll=True)
         shift(state_b)
-        lax.fori_loop(0, chunks, functools.partial(update, state_b, state_a), 0, unroll=True)
+        if levels == 2:
+            before = {}
+            for i in range(chunks):
+                update(state_b, state_a, i, 0, before)
+        else:
+            lax.fori_loop(0, chunks, functools.partial(update, state_b, state_a), 0, unroll=True)
         return 0
 
     lax.fori_loop(0, NSUB // 2, two_steps, 0)
@@ -503,19 +521,21 @@
     outer = (lane < 4) | (lane >= LANES - 4)
     copies = []
     for f in range(4):
+        tiles = []
         for i in range(CHUNKS):
-            rows = pl.ds(8 * i, 8)
             c = 8 * (i + 1)
-            edge = given(f, jnp.where(place < 8, state[f, 0, c : c + 8], state[f, 1, c : c + 8]))
-            for k in range(LEVELS):
-                block = jnp.where(slot_now == 1, mains[1][f, k, rows], mains[2][f, k, rows])
-                block = jnp.where(slot_now == 0, mains[0][f, k, rows], block)
-                if i == 0:
-                    block = jnp.where(upper, band[f, k, 0:8], block)
-                if i == CHUNKS - 1:
-                    block = jnp.where(upper, block, band[f, k, 8:16])
-                merged[f, k, rows] = jnp.where(outer, lane_roll(edge, -(16 * k + 8)), block)
+            tiles.append(given(f, jnp.where(place < 8, state[f, 0, c : c + 8], state[f, 1, c : c + 8])))
         for n in range(2):
+            for i in range(CHUNKS):
+                rows = pl.ds(8 * i, 8)
+                for k in range(n * LEVELS // 2, (n + 1) * LEVELS // 2):
+                    block = jnp.where(slot_now == 1, mains[1][f, k, rows], mains[2][f, k, rows])
+                    block = jnp.where(slot_now == 0, mains[0][f, k, rows], block)
+                    if i == 0:
+                        block = jnp.where(upper, band[f, k, 0:8], block)
+                    if i == CHUNKS - 1:
+                        block = jnp.where(upper, block, band[f, k, 8:16])
+                    merged[f, k, rows] = jnp.where(outer, lane_roll(tiles[i], -(16 * k + 8)), block)
             half = pl.ds(n * LEVELS // 2, LEVELS // 2)
             copies.append(pltpu.make_async_copy(merged.at[f, half], outs[f].at[half], sent.at[2 * f + n]))
             copies[-1].start()

time: 23.9 us -> 23.9 us (level)
  no operation moved by 1% of the time
where the time goes in v4:
time: 23.9 us; the launch traced here: 23.8 us
  starting transfers between devices  11.3 us (47%)
  Pallas kernels  10.3 us (43%)
  waiting for transfers between devices  1.38 us (6%)
  between operations  0.77 us (3%)
    ppermute x1, starting transfers between devices, on_device(): from_b = lax.ppermute(pack_rows(args), AXES, route_b)  7.92 us
    pallas_call x1, Pallas kernels, second_block(): pl.pallas_call(second_body, out_shape=[MAIN, jax.ShapeDtypeStruct((8, LAN...  4.33 us
    ppermute x1, starting transfers between devices, on_device(): from_b = lax.ppermute(to_b, 'lon', route_b)  3.25 us
    pallas_call x1, Pallas kernels, strips_and_merge(): pl.pallas_call(strips_body, out_specs=[pl.BlockSpec(memory_space=pl.ANY)]...  2.59 us
    pallas_call x1, Pallas kernels, third_block(): pl.pallas_call(third_body, out_shape=[MAIN, jax.ShapeDtypeStruct((4, LEVE...  1.69 us
    pallas_call x1, Pallas kernels, pack_rows(): pl.pallas_call(pack_rows_body, in_specs=[pl.BlockSpec(memory_space=pltpu....  0.99 us
    ppermute x1, waiting for transfers between devices, on_device(): from_b = lax.ppermute(to_b, 'lon', route_b)  0.72 us
    ppermute x1, waiting for transfers between devices, on_device(): from_a = lax.ppermute(to_a, AXES, route_a)  0.66 us
  transfers between devices with their start and end apart: 4, of which 2 were waited for; matrix products, arithmetic and copies ran while one was open for 0% of the time, Pallas kernels for 27%

profile of v4, /device:TPU:22, one launch (start us, length us, event | category | flops | bytes accessed | tf_op | source)
XLA Modules:
  0.0 23.8 jit_solution(16382554264172181911)
XLA Ops:
  0.6 0.0 copy-start.4
  0.6 0.0 copy-start.3
  0.7 0.0 copy-start.2
  0.7 0.0 copy-start.1
  0.7 0.0 copy-start
  0.7 1.0 %pack_rows.1 = f32[5,4,8,128]{3,2,1,0:T(8,128)S(1)} custom-call(f32[8,64,128]{2,1,0:T(8,128)} %refs_0_.7, f32[8,64,128]{2,1,0:T(8,128)} %refs_1_.7, f32[8,64,128]{2,1,0:T(8,128)} %refs_2_.7, f32[8,64,128]{2,1,0:T(8,128)} %refs_3_.7, s32[8,64,128]{2,1,0:T(8,128)} %refs_4_.7), custom_call_target="tpu_custom_call" | custom-call | tf_op jit(solution)/shard_map/pack_rows/pallas_call | solution.py:112
  1.7 7.9 %collective-permute-start = (f32[5,4,8,128]{3,2,1,0:T(8,128)S(1)}, f32[5,4,8,128]{3,2,1,0:T(8,128)S(1)}, u32[]{:S(2)}, u32[]{:S(2)}) collective-permute-start(f32[5,4,8,128]{3,2,1,0:T(8,128)S(1)} %pack_rows.1), channel_id=1, source_target_pairs={{32,64},{64,32},{96,128},{128,96},{160,192},{192,160},{224,255},{3... | collective-permute-start | bytes 245768 | tf_op jit(solution)/shard_map/ppermute | solution.py:579
  9.6 0.0 copy-done.4
  9.6 0.0 copy-done.3
  9.6 0.0 copy-done.2
  9.6 0.0 copy-done.1
  9.6 0.0 copy-done
  9.7 0.5 %first_block.1 = (f32[4,8,64,128]{3,2,1,0:T(8,128)S(1)}, f32[5,64,128]{2,1,0:T(8,128)S(1)}, f32[10,8,128]{2,1,0:T(8,128)S(1)}, f32[10,8,128]{2,1,0:T(8,128)S(1)}...) custom-call(f32[8,64,128]{2,1,0:T(8,128)S(1)} %copy-done, f32[8,64,128]{2,1,0:T(8,128)S(1)} %copy-done.1, ...), custom_call_target="tpu_custom_call" | custom-call | flops 300000000 | bytes 20000000 | tf_op jit(solution)/shard_map/first_block/pallas_call | solution.py:412
  10.1 0.1 collective-permute-start.1
  10.2 4.3 %second_block.1 = (f32[4,8,64,128]{3,2,1,0:T(8,128)S(1)}, f32[8,128]{1,0:T(8,128)S(1)}) custom-call(f32[8,64,128]{2,1,0:T(8,128)S(1)} %copy-done, f32[8,64,128]{2,1,0:T(8,128)S(1)} %copy-done.1, f32[8,64,128]{2,1,0:T(8,128)S(1)} %copy-done.2, f32[8,64,128]{2,1,0:T(8,128)S(1)} %copy-done.3, s32[8,64,128]{2,1,0:T(8,128)S(1)} %copy-done.4, ...), custom_call_target="tpu_custom_call" | custom-call | flops 300000000 | bytes 20000000 | tf_op jit(solution)/shard_map/second_block/pallas_call | solution.py:439
  14.6 0.0 collective-permute-done.from_b
  14.6 0.7 %collective-permute-done.1.from_a = f32[5,4,8,128]{3,2,1,0:T(8,128)S(1)} collective-permute-done((f32[5,4,8,128]{3,2,1,0:T(8,128)S(1)}, f32[5,4,8,128]{3,2,1,0:T(8,128)S(1)}, u32[]{:S(2)}, u32[]{:S(2)}) %collective-permute-start.1) | collective-permute-done | bytes 81952 | tf_op jit(solution)/shard_map/ppermute | solution.py:581
  15.3 0.3 %assemble.1 = (f32[5,8,8,128]{3,2,1,0:T(8,128)S(1)}, f32[5,8,128]{2,1,0:T(8,128)S(1)}, f32[12,8,128]{2,1,0:T(8,128)S(1)}, f32[12,8,128]{2,1,0:T(8,128)S(1)}) custom-call(f32[5,4,8,128]{3,2,1,0:T(8,128)S(1)} %collective-permute-done.from_b, f32[5,4,8,128]{3,2,1,0:T(8,128)S(1)} %collective-permute-done.1.from_a, f32[10,8,128]{2,1,0:T(8,128)S(1)} %get-tuple-element.20.part_b, ...), custom_call_target="tpu_custom_call" | custom-call | tf_op jit(solution)/shard_map/assemble/pallas_call | solution.py:231
  15.5 3.2 %collective-permute-start.2 = (f32[12,8,128]{2,1,0:T(8,128)S(1)}, f32[12,8,128]{2,1,0:T(8,128)S(1)}, u32[]{:S(2)}, u32[]{:S(2)}) collective-permute-start(f32[12,8,128]{2,1,0:T(8,128)S(1)} %get-tuple-element.24), channel_id=1, source_target_pairs={{0,31},{1,2},{2,1},{3,4},{4,3},{5,6},{6,5},{7,8},{8,7},{9,10},{10,... | collective-permute-start | bytes 147464 | tf_op jit(solution)/shard_map/ppermute | solution.py:585
  18.8 0.0 collective-permute-start.3
  18.8 1.7 %third_block.1 = (f32[4,8,64,128]{3,2,1,0:T(8,128)S(1)}, f32[4,8,16,128]{3,2,1,0:T(8,128)S(1)}) custom-call(f32[8,64,128]{2,1,0:T(8,128)S(1)} %copy-done, f32[8,64,128]{2,1,0:T(8,128)S(1)} %copy-done.1, f32[8,64,128]{2,1,0:T(8,128)S(1)} %copy-done.2, f32[8,64,128]{2,1,0:T(8,128)S(1)} %copy-done.3, s32[8,64,128]{2,1,0:T(8,128)S(1)} %copy-done.4, ...), custom_call_target="tpu_custom_call" | custom-call | flops 200000000 | bytes 10000000 | tf_op jit(solution)/shard_map/third_block/pallas_call | solution.py:461
  20.5 0.7 %collective-permute-done.2.from_b = f32[12,8,128]{2,1,0:T(8,128)S(1)} collective-permute-done((f32[12,8,128]{2,1,0:T(8,128)S(1)}, f32[12,8,128]{2,1,0:T(8,128)S(1)}, u32[]{:S(2)}, u32[]{:S(2)}) %collective-permute-start.2) | collective-permute-done | bytes 49184 | tf_op jit(solution)/shard_map/ppermute | solution.py:585
  21.2 0.0 collective-permute-done.3.from_a
  21.2 2.6 %strips_and_merge.1 = (f32[8,64,128]{2,1,0:T(8,128)}, f32[8,64,128]{2,1,0:T(8,128)}, f32[8,64,128]{2,1,0:T(8,128)}, f32[8,64,128]{2,1,0:T(8,128)}) custom-call(f32[5,64,128]{2,1,0:T(8,128)S(1)} %get-tuple-element.18.refs_5_.edges, f32[5,8,128]{2,1,0:T(8,128)S(1)} %get-tuple-element.23.edge_halo, f32[12,8,128]{2,1,0:T(8,128)S(1)} %collective-permute-done.2.from_b, ...), custom_call_target="tpu_custom_call" | custom-call | tf_op jit(solution)/shard_map/strips_and_merge/pallas_call | solution.py:548
Async XLA Ops:
  0.6 9.0 %copy-start.4 = (s32[8,64,128]{2,1,0:T(8,128)S(1)}, s32[8,64,128]{2,1,0:T(8,128)}, u32[]{:S(2)}) copy-start(s32[8,64,128]{2,1,0:T(8,128)} %refs_4_.7) | copy-start | bytes 786436
  0.6 9.0 %copy-start.3 = (f32[8,64,128]{2,1,0:T(8,128)S(1)}, f32[8,64,128]{2,1,0:T(8,128)}, u32[]{:S(2)}) copy-start(f32[8,64,128]{2,1,0:T(8,128)} %refs_3_.7) | copy-start | bytes 786436
  0.7 9.0 %copy-start.2 = (f32[8,64,128]{2,1,0:T(8,128)S(1)}, f32[8,64,128]{2,1,0:T(8,128)}, u32[]{:S(2)}) copy-start(f32[8,64,128]{2,1,0:T(8,128)} %refs_2_.7) | copy-start | bytes 786436
  0.7 9.0 %copy-start.1 = (f32[8,64,128]{2,1,0:T(8,128)S(1)}, f32[8,64,128]{2,1,0:T(8,128)}, u32[]{:S(2)}) copy-start(f32[8,64,128]{2,1,0:T(8,128)} %refs_1_.7) | copy-start | bytes 786436
  0.7 9.0 %copy-start = (f32[8,64,128]{2,1,0:T(8,128)S(1)}, f32[8,64,128]{2,1,0:T(8,128)}, u32[]{:S(2)}) copy-start(f32[8,64,128]{2,1,0:T(8,128)} %refs_0_.7) | copy-start | bytes 786436
  1.7 12.9 %collective-permute-start = (f32[5,4,8,128]{3,2,1,0:T(8,128)S(1)}, f32[5,4,8,128]{3,2,1,0:T(8,128)S(1)}, u32[]{:S(2)}, u32[]{:S(2)}) collective-permute-start(f32[5,4,8,128]{3,2,1,0:T(8,128)S(1)} %pack_rows.1), channel_id=1, source_target_pairs={{32,64},{64,32},{96,128},{128,96},{160,192},{192,160},{224,255},{3... | collective-permute-start | bytes 245768 | tf_op jit(solution)/shard_map/ppermute | solution.py:579
  10.1 5.1 %collective-permute-start.1 = (f32[5,4,8,128]{3,2,1,0:T(8,128)S(1)}, f32[5,4,8,128]{3,2,1,0:T(8,128)S(1)}, u32[]{:S(2)}, u32[]{:S(2)}) collective-permute-start(f32[5,4,8,128]{3,2,1,0:T(8,128)S(1)} %get-tuple-element.19), channel_id=1, source_target_pairs={{0,32},{32,0},{64,96},{96,64},{128,160},{160,128},{192,224},{224,1... | collective-permute-start | bytes 245768 | tf_op jit(solution)/shard_map/ppermute | solution.py:581
  15.5 5.7 %collective-permute-start.2 = (f32[12,8,128]{2,1,0:T(8,128)S(1)}, f32[12,8,128]{2,1,0:T(8,128)S(1)}, u32[]{:S(2)}, u32[]{:S(2)}) collective-permute-start(f32[12,8,128]{2,1,0:T(8,128)S(1)} %get-tuple-element.24), channel_id=1, source_target_pairs={{0,31},{1,2},{2,1},{3,4},{4,3},{5,6},{6,5},{7,8},{8,7},{9,10},{10,... | collective-permute-start | bytes 147464 | tf_op jit(solution)/shard_map/ppermute | solution.py:585
  18.8 2.4 %collective-permute-start.3 = (f32[12,8,128]{2,1,0:T(8,128)S(1)}, f32[12,8,128]{2,1,0:T(8,128)S(1)}, u32[]{:S(2)}, u32[]{:S(2)}) collective-permute-start(f32[12,8,128]{2,1,0:T(8,128)S(1)} %get-tuple-element.25), channel_id=1, source_target_pairs={{0,1},{1,0},{2,3},{3,2},{4,5},{5,4},{6,7},{7,6},{8,9},{9,8},{10,11... | collective-permute-start | bytes 147464 | tf_op jit(solution)/shard_map/ppermute | solution.py:586

commit v5 on v3

--- a/solution.py
+++ b/solution.py
@@ -101,11 +101,13 @@
         copies.append(pltpu.make_async_copy(fields[f].at[:, pl.ds(start, 8), :], target, arrived.at[f]))
     for copy in copies:
         copy.start()
-    for copy in copies:
-        copy.wait()
-    pack_pairs(
-        lambda f, k: held_rows[f, k] if f < 4 else held_mask[k].astype(jnp.float32), odd_lat(), out
-    )
+
+    def take(f, k):
+        if k == 0:
+            copies[f].wait()
+        return held_rows[f, k] if f < 4 else held_mask[k].astype(jnp.float32)
+
+    pack_pairs(take, odd_lat(), out)
 
 
 def pack_rows(fields):

time: 23.9 us -> 23.9 us (level)
  no operation moved by 1% of the time
where the time goes in v5:
time: 23.9 us; the launch traced here: 23.8 us
  starting transfers between devices  11.3 us (47%)
  Pallas kernels  10.4 us (44%)
  waiting for transfers between devices  1.38 us (6%)
  between operations  0.77 us (3%)
    ppermute x1, starting transfers between devices, on_device(): from_b = lax.ppermute(pack_rows(args), AXES, route_b)  7.92 us
    pallas_call x1, Pallas kernels, second_block(): pl.pallas_call(second_body, out_shape=[MAIN, jax.ShapeDtypeStruct((8, LAN...  4.33 us
    ppermute x1, starting transfers between devices, on_device(): from_b = lax.ppermute(to_b, 'lon', route_b)  3.25 us
    pallas_call x1, Pallas kernels, strips_and_merge(): pl.pallas_call(strips_body, out_specs=[pl.BlockSpec(memory_space=pl.ANY)]...  2.63 us
    pallas_call x1, Pallas kernels, third_block(): pl.pallas_call(third_body, out_shape=[MAIN, jax.ShapeDtypeStruct((4, LEVE...  1.69 us
    pallas_call x1, Pallas kernels, pack_rows(): pl.pallas_call(pack_rows_body, in_specs=[pl.BlockSpec(memory_space=pltpu....  0.98 us
    ppermute x1, waiting for transfers between devices, on_device(): from_b = lax.ppermute(to_b, 'lon', route_b)  0.72 us
    ppermute x1, waiting for transfers between devices, on_device(): from_a = lax.ppermute(to_a, AXES, route_a)  0.66 us
  transfers between devices with their start and end apart: 4, of which 2 were waited for; matrix products, arithmetic and copies ran while one was open for 0% of the time, Pallas kernels for 27%

profile of v5, /device:TPU:22, one launch (start us, length us, event | category | flops | bytes accessed | tf_op | source)
XLA Modules:
  0.0 23.8 jit_solution(13546503646553538890)
XLA Ops:
  0.6 0.0 copy-start.4
  0.6 0.0 copy-start.3
  0.7 0.0 copy-start.2
  0.7 0.0 copy-start.1
  0.7 0.0 copy-start
  0.7 1.0 %pack_rows.1 = f32[5,4,8,128]{3,2,1,0:T(8,128)S(1)} custom-call(f32[8,64,128]{2,1,0:T(8,128)} %refs_0_.7, f32[8,64,128]{2,1,0:T(8,128)} %refs_1_.7, f32[8,64,128]{2,1,0:T(8,128)} %refs_2_.7, f32[8,64,128]{2,1,0:T(8,128)} %refs_3_.7, s32[8,64,128]{2,1,0:T(8,128)} %refs_4_.7), custom_call_target="tpu_custom_call" | custom-call | tf_op jit(solution)/shard_map/pack_rows/pallas_call | solution.py:114
  1.7 7.9 %collective-permute-start = (f32[5,4,8,128]{3,2,1,0:T(8,128)S(1)}, f32[5,4,8,128]{3,2,1,0:T(8,128)S(1)}, u32[]{:S(2)}, u32[]{:S(2)}) collective-permute-start(f32[5,4,8,128]{3,2,1,0:T(8,128)S(1)} %pack_rows.1), channel_id=1, source_target_pairs={{32,64},{64,32},{96,128},{128,96},{160,192},{192,160},{224,255},{3... | collective-permute-start | bytes 245768 | tf_op jit(solution)/shard_map/ppermute | solution.py:561
  9.6 0.0 copy-done.4
  9.6 0.0 copy-done.3
  9.6 0.0 copy-done.2
  9.6 0.0 copy-done.1
  9.6 0.0 copy-done
  9.6 0.5 %first_block.1 = (f32[4,8,64,128]{3,2,1,0:T(8,128)S(1)}, f32[5,64,128]{2,1,0:T(8,128)S(1)}, f32[10,8,128]{2,1,0:T(8,128)S(1)}, f32[10,8,128]{2,1,0:T(8,128)S(1)}...) custom-call(f32[8,64,128]{2,1,0:T(8,128)S(1)} %copy-done, f32[8,64,128]{2,1,0:T(8,128)S(1)} %copy-done.1, ...), custom_call_target="tpu_custom_call" | custom-call | flops 300000000 | bytes 20000000 | tf_op jit(solution)/shard_map/first_block/pallas_call | solution.py:396
  10.1 0.1 collective-permute-start.1
  10.2 4.3 %second_block.1 = (f32[4,8,64,128]{3,2,1,0:T(8,128)S(1)}, f32[8,128]{1,0:T(8,128)S(1)}) custom-call(f32[8,64,128]{2,1,0:T(8,128)S(1)} %copy-done, f32[8,64,128]{2,1,0:T(8,128)S(1)} %copy-done.1, f32[8,64,128]{2,1,0:T(8,128)S(1)} %copy-done.2, f32[8,64,128]{2,1,0:T(8,128)S(1)} %copy-done.3, s32[8,64,128]{2,1,0:T(8,128)S(1)} %copy-done.4, ...), custom_call_target="tpu_custom_call" | custom-call | flops 300000000 | bytes 20000000 | tf_op jit(solution)/shard_map/second_block/pallas_call | solution.py:423
  14.6 0.0 collective-permute-done.from_b
  14.6 0.7 %collective-permute-done.1.from_a = f32[5,4,8,128]{3,2,1,0:T(8,128)S(1)} collective-permute-done((f32[5,4,8,128]{3,2,1,0:T(8,128)S(1)}, f32[5,4,8,128]{3,2,1,0:T(8,128)S(1)}, u32[]{:S(2)}, u32[]{:S(2)}) %collective-permute-start.1) | collective-permute-done | bytes 81952 | tf_op jit(solution)/shard_map/ppermute | solution.py:563
  15.2 0.3 %assemble.1 = (f32[5,8,8,128]{3,2,1,0:T(8,128)S(1)}, f32[5,8,128]{2,1,0:T(8,128)S(1)}, f32[12,8,128]{2,1,0:T(8,128)S(1)}, f32[12,8,128]{2,1,0:T(8,128)S(1)}) custom-call(f32[5,4,8,128]{3,2,1,0:T(8,128)S(1)} %collective-permute-done.from_b, f32[5,4,8,128]{3,2,1,0:T(8,128)S(1)} %collective-permute-done.1.from_a, f32[10,8,128]{2,1,0:T(8,128)S(1)} %get-tuple-element.20.part_b, ...), custom_call_target="tpu_custom_call" | custom-call | tf_op jit(solution)/shard_map/assemble/pallas_call | solution.py:233
  15.5 3.2 %collective-permute-start.2 = (f32[12,8,128]{2,1,0:T(8,128)S(1)}, f32[12,8,128]{2,1,0:T(8,128)S(1)}, u32[]{:S(2)}, u32[]{:S(2)}) collective-permute-start(f32[12,8,128]{2,1,0:T(8,128)S(1)} %get-tuple-element.24), channel_id=1, source_target_pairs={{0,31},{1,2},{2,1},{3,4},{4,3},{5,6},{6,5},{7,8},{8,7},{9,10},{10,... | collective-permute-start | bytes 147464 | tf_op jit(solution)/shard_map/ppermute | solution.py:567
  18.8 0.0 collective-permute-start.3
  18.8 1.7 %third_block.1 = (f32[4,8,64,128]{3,2,1,0:T(8,128)S(1)}, f32[4,8,16,128]{3,2,1,0:T(8,128)S(1)}) custom-call(f32[8,64,128]{2,1,0:T(8,128)S(1)} %copy-done, f32[8,64,128]{2,1,0:T(8,128)S(1)} %copy-done.1, f32[8,64,128]{2,1,0:T(8,128)S(1)} %copy-done.2, f32[8,64,128]{2,1,0:T(8,128)S(1)} %copy-done.3, s32[8,64,128]{2,1,0:T(8,128)S(1)} %copy-done.4, ...), custom_call_target="tpu_custom_call" | custom-call | flops 200000000 | bytes 10000000 | tf_op jit(solution)/shard_map/third_block/pallas_call | solution.py:445
  20.5 0.7 %collective-permute-done.2.from_b = f32[12,8,128]{2,1,0:T(8,128)S(1)} collective-permute-done((f32[12,8,128]{2,1,0:T(8,128)S(1)}, f32[12,8,128]{2,1,0:T(8,128)S(1)}, u32[]{:S(2)}, u32[]{:S(2)}) %collective-permute-start.2) | collective-permute-done | bytes 49184 | tf_op jit(solution)/shard_map/ppermute | solution.py:567
  21.2 0.0 collective-permute-done.3.from_a
  21.2 2.6 %strips_and_merge.1 = (f32[8,64,128]{2,1,0:T(8,128)}, f32[8,64,128]{2,1,0:T(8,128)}, f32[8,64,128]{2,1,0:T(8,128)}, f32[8,64,128]{2,1,0:T(8,128)}) custom-call(f32[5,64,128]{2,1,0:T(8,128)S(1)} %get-tuple-element.18.refs_5_.edges, f32[5,8,128]{2,1,0:T(8,128)S(1)} %get-tuple-element.23.edge_halo, f32[12,8,128]{2,1,0:T(8,128)S(1)} %collective-permute-done.2.from_b, ...), custom_call_target="tpu_custom_call" | custom-call | tf_op jit(solution)/shard_map/strips_and_merge/pallas_call | solution.py:530
Async XLA Ops:
  0.6 9.0 %copy-start.4 = (s32[8,64,128]{2,1,0:T(8,128)S(1)}, s32[8,64,128]{2,1,0:T(8,128)}, u32[]{:S(2)}) copy-start(s32[8,64,128]{2,1,0:T(8,128)} %refs_4_.7) | copy-start | bytes 786436
  0.6 9.0 %copy-start.3 = (f32[8,64,128]{2,1,0:T(8,128)S(1)}, f32[8,64,128]{2,1,0:T(8,128)}, u32[]{:S(2)}) copy-start(f32[8,64,128]{2,1,0:T(8,128)} %refs_3_.7) | copy-start | bytes 786436
  0.7 9.0 %copy-start.2 = (f32[8,64,128]{2,1,0:T(8,128)S(1)}, f32[8,64,128]{2,1,0:T(8,128)}, u32[]{:S(2)}) copy-start(f32[8,64,128]{2,1,0:T(8,128)} %refs_2_.7) | copy-start | bytes 786436
  0.7 9.0 %copy-start.1 = (f32[8,64,128]{2,1,0:T(8,128)S(1)}, f32[8,64,128]{2,1,0:T(8,128)}, u32[]{:S(2)}) copy-start(f32[8,64,128]{2,1,0:T(8,128)} %refs_1_.7) | copy-start | bytes 786436
  0.7 9.0 %copy-start = (f32[8,64,128]{2,1,0:T(8,128)S(1)}, f32[8,64,128]{2,1,0:T(8,128)}, u32[]{:S(2)}) copy-start(f32[8,64,128]{2,1,0:T(8,128)} %refs_0_.7) | copy-start | bytes 786436
  1.7 12.9 %collective-permute-start = (f32[5,4,8,128]{3,2,1,0:T(8,128)S(1)}, f32[5,4,8,128]{3,2,1,0:T(8,128)S(1)}, u32[]{:S(2)}, u32[]{:S(2)}) collective-permute-start(f32[5,4,8,128]{3,2,1,0:T(8,128)S(1)} %pack_rows.1), channel_id=1, source_target_pairs={{32,64},{64,32},{96,128},{128,96},{160,192},{192,160},{224,255},{3... | collective-permute-start | bytes 245768 | tf_op jit(solution)/shard_map/ppermute | solution.py:561
  10.1 5.1 %collective-permute-start.1 = (f32[5,4,8,128]{3,2,1,0:T(8,128)S(1)}, f32[5,4,8,128]{3,2,1,0:T(8,128)S(1)}, u32[]{:S(2)}, u32[]{:S(2)}) collective-permute-start(f32[5,4,8,128]{3,2,1,0:T(8,128)S(1)} %get-tuple-element.19), channel_id=1, source_target_pairs={{0,32},{32,0},{64,96},{96,64},{128,160},{160,128},{192,224},{224,1... | collective-permute-start | bytes 245768 | tf_op jit(solution)/shard_map/ppermute | solution.py:563
  15.5 5.7 %collective-permute-start.2 = (f32[12,8,128]{2,1,0:T(8,128)S(1)}, f32[12,8,128]{2,1,0:T(8,128)S(1)}, u32[]{:S(2)}, u32[]{:S(2)}) collective-permute-start(f32[12,8,128]{2,1,0:T(8,128)S(1)} %get-tuple-element.24), channel_id=1, source_target_pairs={{0,31},{1,2},{2,1},{3,4},{4,3},{5,6},{6,5},{7,8},{8,7},{9,10},{10,... | collective-permute-start | bytes 147464 | tf_op jit(solution)/shard_map/ppermute | solution.py:567
  18.8 2.4 %collective-permute-start.3 = (f32[12,8,128]{2,1,0:T(8,128)S(1)}, f32[12,8,128]{2,1,0:T(8,128)S(1)}, u32[]{:S(2)}, u32[]{:S(2)}) collective-permute-start(f32[12,8,128]{2,1,0:T(8,128)S(1)} %get-tuple-element.25), channel_id=1, source_target_pairs={{0,1},{1,0},{2,3},{3,2},{4,5},{5,4},{6,7},{7,6},{8,9},{9,8},{10,11... | collective-permute-start | bytes 147464 | tf_op jit(solution)/shard_map/ppermute | solution.py:568
